TPU v7x, 32 devices: a whole 2x2x4 slice. The times are simulated.
32 devices in a mesh: energy: 16 (over z, x, core), slab: 2 (over y).
Axes of the slice: x: 2, y: 2, z: 4, core: 2. Of those that a mesh axis runs over, the one named last changes fastest.
Arguments:
- green_blocks: bfloat16 [2, 12, 12, 256, 128], P(None, None, None, 'energy', 'slab'), may hold values from -6 to 6
- couplings: bfloat16 [12, 12, 2, 1024], P(None, None, 'slab', 'energy'), may hold values from -1.75 to 1.75
- band_weights: float32 [9, 2, 1024], P(None, 'slab', 'energy'), may hold values from 0.02 to 0.2
- neighbours: int32 [2, 1024], P('slab', 'energy'), may hold values from 0 to 127, as said below
- shifts: int32 [2, 1024], P('slab', 'energy'), may hold values from -32 to 32
Outputs:
- self_energy: bfloat16 [2, 12, 12, 256, 128], P(None, None, None, 'energy', 'slab')
Inputs may be any that keep to these rules, and one draw needn't show every extreme that they name: `neighbours`: the partner of each coupling of atom a lies within 4 atoms of a; partners of one atom may repeat.
All inputs are finite; a program needn't handle non-finite values.
Results may differ from a plain program's by a relative error of at most 0.0057.
Values may be sent and summed in bfloat16 or wider, within the bound.
A program may use at most 128 MiB of HBM per device.

v0:
```python
import functools

import jax
import jax.numpy as jnp
from jax import lax
from jax.experimental import pallas as pl
from jax.experimental.pallas import tpu as pltpu
from jax.sharding import PartitionSpec as P

ORB = 12
NBR = 16
BAND = 9
SHIFT = 32
HALO = 4
BLOCK = 2 * ORB * ORB
PAIR = ORB * ORB


MESH = pl.DeviceIdType.MESH


def order(groups, per_dev):
    count = groups * per_dev
    row = lax.broadcasted_iota(jnp.int32, (count, count), 0)
    atom = lax.broadcasted_iota(jnp.int32, (count, count), 1)
    return (atom == (row % groups) * per_dev + row // groups).astype(jnp.bfloat16)


def pack_kernel(groups, per_dev, x_ref, sent, wide, packed):
    local_e = sent.shape[1]
    tiles = wide.shape[0]
    count = x_ref.shape[1]
    lanes = min(count, 128)
    if lanes < 128:
        wide[...] = jnp.zeros_like(wide)
    for j in range(tiles):
        wide[j, :x_ref.shape[0], :lanes] = x_ref[:, j * 128:j * 128 + lanes].astype(jnp.float32)
    pick = order(groups, per_dev)
    for e in range(local_e):
        rows = jnp.concatenate([wide[j, pl.ds(e, BLOCK, stride=local_e), :] for j in range(tiles)], axis=1)
        rows = rows[:, :count].astype(jnp.bfloat16)
        turned = lax.dot_general(pick, rows, (((1,), (1,)), ((), ())), preferred_element_type=jnp.float32)
        flat = jnp.concatenate([turned[i * groups:(i + 1) * groups] for i in range(per_dev)], axis=1)
        for j in range(packed.shape[0]):
            packed[j, pl.ds(e, groups, stride=local_e), :] = flat[:, j * 128:(j + 1) * 128]
    for g in range(groups):
        for j in range(packed.shape[0]):
            sent[g, :, j * 128:(j + 1) * 128] = packed[j, g * local_e:(g + 1) * local_e, :].astype(jnp.bfloat16)


def gather_kernel(groups, x_ref, landed, send_sem, recv_sem):
    me, slab = lax.axis_index("energy"), lax.axis_index("slab")
    barrier = pltpu.get_barrier_semaphore()

    def hello(step, carry):
        pl.semaphore_signal(barrier, inc=1, device_id=(lax.rem(me + step, groups), slab), device_id_type=MESH)
        return carry

    lax.fori_loop(1, groups, hello, 0)
    pl.semaphore_wait(barrier, groups - 1)

    def outgoing(step):
        to = lax.rem(me + step, groups)
        return pltpu.make_async_remote_copy(
            src_ref=x_ref.at[to], dst_ref=landed.at[me], send_sem=send_sem.at[step], recv_sem=recv_sem.at[step],
            device_id=(to, slab), device_id_type=MESH)

    def incoming(step):
        source = lax.rem(me - step + groups, groups)
        return pltpu.make_async_remote_copy(
            src_ref=x_ref.at[source], dst_ref=landed.at[source], send_sem=send_sem.at[step],
            recv_sem=recv_sem.at[step], device_id=(source, slab), device_id_type=MESH)

    def start(step, carry):
        outgoing(step).start()
        return carry

    def finish(step, carry):
        incoming(step).wait_recv()
        outgoing(step).wait_send()
        return carry

    lax.fori_loop(1, groups, start, 0)
    landed[me] = x_ref[me]
    lax.fori_loop(1, groups, finish, 0)


def unpack_kernel(groups, per_dev, landed, out_ref, wide, tall):
    local_e = landed.shape[1]
    lanes = min(out_ref.shape[1], 128)
    for g in range(groups):
        for j in range(wide.shape[0]):
            wide[j, g * local_e:(g + 1) * local_e, :] = landed[g, :, j * 128:(j + 1) * 128].astype(jnp.float32)
    pick = order(groups, per_dev)
    for e in range(local_e):
        rows = jnp.concatenate(
            [wide[j, pl.ds(e, groups, stride=local_e), :] for j in range(wide.shape[0])], axis=1)
        stack = jnp.concatenate([rows[:, i * BLOCK:(i + 1) * BLOCK] for i in range(per_dev)], axis=0)
        turned = jnp.dot(stack.T.astype(jnp.bfloat16), pick, preferred_element_type=jnp.float32)
        if lanes < 128:
            turned = jnp.concatenate([turned, jnp.zeros((BLOCK, 128 - lanes), jnp.float32)], axis=1)
        for j in range(tall.shape[0]):
            tall[j, pl.ds(e, BLOCK, stride=local_e), :] = turned[:, j * 128:(j + 1) * 128]
    for j in range(tall.shape[0]):
        out_ref[:, j * 128:j * 128 + lanes] = tall[j, :out_ref.shape[0], :lanes].astype(jnp.bfloat16)


def scatter_kernel(near_ref, shift_ref, left_ref, own_ref, right_ref, weight_ref, matrix_ref, out_ref,
                   green, spread_q, spread_r, total):
    per_dev = out_ref.shape[1] // BLOCK
    energies = out_ref.shape[0]
    half = energies // 2
    width = per_dev * BLOCK
    groups = lax.axis_size("energy")
    first_atom = (lax.axis_index("slab") * groups + lax.axis_index("energy")) * per_dev - HALO

    for place, ref in enumerate((left_ref, own_ref, right_ref)):
        green[place * width:(place + 1) * width, :] = ref[...].T

    lane_q = lax.broadcasted_iota(jnp.int32, (128, PAIR), 1)
    row_q = lax.broadcasted_iota(jnp.int32, (128, PAIR), 0)
    pick_q = (lane_q // ORB == row_q).astype(jnp.bfloat16)
    pick_r = (lane_q % ORB == row_q).astype(jnp.bfloat16)
    spread_q[...] = jnp.dot(matrix_ref[...], pick_q, preferred_element_type=jnp.float32).astype(jnp.bfloat16)
    spread_r[...] = jnp.dot(matrix_ref[...], pick_r, preferred_element_type=jnp.float32).astype(jnp.bfloat16)
    row_p = lax.broadcasted_iota(jnp.int32, (PAIR, 16), 0)
    lane_p = lax.broadcasted_iota(jnp.int32, (PAIR, 16), 1)
    pick_p = (row_p // ORB == lane_p).astype(jnp.bfloat16)
    pick_t = (row_p % ORB == lane_p).astype(jnp.bfloat16)
    below = lax.broadcasted_iota(jnp.int32, (half, half), 0) > lax.broadcasted_iota(jnp.int32, (half, half), 1)
    above = lax.broadcasted_iota(jnp.int32, (half, half), 0) < lax.broadcasted_iota(jnp.int32, (half, half), 1)

    sub = lax.broadcasted_iota(jnp.int32, (8, energies), 0)

    def atom(a, carry):
        held = [None, None]
        for k in range(NBR):
            index = a * NBR + k
            row = weight_ref[pl.ds(index, 1), :]
            turn = lax.rem(2 * energies - BAND // 2 - shift_ref[0, index], energies)
            tile = pltpu.roll(jnp.broadcast_to(row, (8, energies)), turn, 1)
            for step in (1, 2, 4):
                tile = jnp.where((sub & step) != 0, pltpu.roll(tile, step, 1), tile)
            band = jnp.concatenate([pltpu.roll(tile, 8 * b, 1) if b else tile for b in range(half // 8)], axis=0)
            near, far = band[:, :half], band[:, half:]
            near = near.astype(jnp.bfloat16)
            upper = jnp.where(below, far, 0.0).astype(jnp.bfloat16)
            lower = jnp.where(above, far, 0.0).astype(jnp.bfloat16)
            toeplitz = jnp.concatenate([
                jnp.concatenate([near, upper], axis=1),
                jnp.concatenate([lower, near], axis=1)], axis=0)
            partner = jnp.clip(near_ref[0, index] - first_atom, 0, 3 * per_dev - 1)
            block = green[pl.ds(pl.multiple_of(partner * BLOCK, 32), BLOCK), :]
            banded = jnp.dot(block, toeplitz, preferred_element_type=jnp.float32).astype(jnp.bfloat16)
            rows = pl.ds(pl.multiple_of(index * 16, 16), 16)
            left = jnp.dot(pick_p, spread_q[rows, :], preferred_element_type=jnp.float32)
            right = jnp.dot(pick_t, spread_r[rows, :], preferred_element_type=jnp.float32)
            both = (left * right).astype(jnp.bfloat16)
            for c in range(2):
                part = slice(c * PAIR, (c + 1) * PAIR)
                term = jnp.dot(both, banded[part], preferred_element_type=jnp.float32)
                if k % 2 == 0:
                    held[c] = term
                elif k == 1:
                    total[part, :] = held[c] + term
                else:
                    total[part, :] += held[c] + term
        return carry

    for a in range(per_dev):
        atom(a, 0)
        out_ref[:, a * BLOCK:(a + 1) * BLOCK] = total[...].T.astype(jnp.bfloat16)


def on_device(green_blocks, couplings, band_weights, neighbours, shifts):
    groups = lax.axis_size("energy")
    slabs = lax.axis_size("slab")
    local_e, slab_count = green_blocks.shape[3:]
    per_dev = slab_count // groups
    energies = local_e * groups
    width = per_dev * BLOCK
    pairs = per_dev * NBR
    assert per_dev == HALO
    vmem = pl.BlockSpec(memory_space=pltpu.VMEM)
    smem = pl.BlockSpec(memory_space=pltpu.SMEM)
    blocks = jax.ShapeDtypeStruct((groups, local_e, width), jnp.bfloat16)
    wide = pltpu.VMEM((pl.cdiv(slab_count, 128), BLOCK * local_e, 128), jnp.float32)
    packed = pltpu.VMEM((width // 128, energies, 128), jnp.float32)
    room = pltpu.CompilerParams(vmem_limit_bytes=32 * 1024 * 1024)
    sent = pl.pallas_call(
        functools.partial(pack_kernel, groups, per_dev),
        out_shape=blocks, in_specs=[vmem], out_specs=vmem,
        scratch_shapes=[wide, packed], compiler_params=room,
    )(green_blocks.reshape(BLOCK * local_e, slab_count))
    def exchanged(value, number):
        return pl.pallas_call(
            functools.partial(gather_kernel, groups),
            out_shape=blocks,
            in_specs=[vmem],
            out_specs=vmem,
            scratch_shapes=[
                pltpu.SemaphoreType.DMA((groups,)),
                pltpu.SemaphoreType.DMA((groups,)),
            ],
            compiler_params=pltpu.CompilerParams(
                collective_id=number, has_side_effects=True, vmem_limit_bytes=32 * 1024 * 1024),
        )(value)

    own = exchanged(sent, 0).reshape(energies, width)
    chain = [g * slabs + s for s in range(slabs) for g in range(groups)]
    up = list(zip(chain[:-1], chain[1:]))
    left = lax.ppermute(own, ("energy", "slab"), up)
    right = lax.ppermute(own, ("energy", "slab"), [(j, i) for i, j in up])

    weight = jnp.pad(band_weights.reshape(BAND, pairs)[::-1].T, ((0, 0), (0, energies - BAND)))
    matrix = couplings.reshape(ORB, ORB, pairs).transpose(2, 0, 1)
    matrix = jnp.pad(matrix, ((0, 0), (0, 16 - ORB), (0, 128 - ORB))).reshape(pairs * 16, 128)
    out = pl.pallas_call(
        scatter_kernel,
        out_shape=jax.ShapeDtypeStruct((energies, width), jnp.bfloat16),
        in_specs=[smem, smem, vmem, vmem, vmem, vmem, vmem],
        out_specs=vmem,
        scratch_shapes=[
            pltpu.VMEM((3 * width, energies), jnp.bfloat16),
            pltpu.VMEM((pairs * 16, PAIR), jnp.bfloat16),
            pltpu.VMEM((pairs * 16, PAIR), jnp.bfloat16),
            pltpu.VMEM((BLOCK, energies), jnp.float32),
        ],
        compiler_params=pltpu.CompilerParams(vmem_limit_bytes=40 * 1024 * 1024),
    )(neighbours, shifts, left, own, right, weight, matrix)
    landed = exchanged(out.reshape(groups, local_e, width), 1)
    back = pl.pallas_call(
        functools.partial(unpack_kernel, groups, per_dev),
        out_shape=jax.ShapeDtypeStruct((BLOCK * local_e, slab_count), jnp.bfloat16),
        in_specs=[vmem], out_specs=vmem,
        scratch_shapes=[packed, wide], compiler_params=room,
    )(landed)
    return back.reshape(2, ORB, ORB, local_e, slab_count)


def solution(mesh):
    return jax.shard_map(
        on_device,
        mesh=mesh,
        in_specs=(
            P(None, None, None, "energy", "slab"),
            P(None, None, "slab", "energy"),
            P(None, "slab", "energy"),
            P("slab", "energy"),
            P("slab", "energy"),
        ),
        out_specs=P(None, None, None, "energy", "slab"),
        check_vma=False,
    )
```

profile of v0, /device:TPU:15, one launch (start us, length us, event | category | flops | bytes accessed | tf_op | source)
XLA Modules:
  0.0 77.4 jit_solution(13929006524839172725)
XLA Ops:
  0.0 0.0 copy-start
  0.0 1.3 %copy-done = bf16[2,12,12,16,64]{4,3,2,1,0:T(8,128)(2,1)S(1)} copy-done((bf16[2,12,12,16,64]{4,3,2,1,0:T(8,128)(2,1)S(1)}, bf16[2,12,12,16,64]{4,3,2,1,0:T(8,128)(2,1)}, u32[]{:S(2)}) %copy-start) | copy-done | bytes 589848
  1.3 0.0 copy-start.4
  1.3 0.0 copy-start.3
  1.3 1.6 %shard_map.55.x_ref = bf16[16,16,1152]{2,1,0:T(8,128)(2,1)S(1)} custom-call(bf16[4608,64]{1,0:T(8,128)(2,1)S(1)} %bitcast.14), custom_call_target="tpu_custom_call" | custom-call | tf_op jit(solution)/shard_map/pallas_call | solution.py:190
  2.9 0.0 copy-start.1
  2.9 0.0 copy-start.2
  2.9 18.2 %shard_map.56 = bf16[16,16,1152]{2,1,0:T(8,128)(2,1)S(1)} custom-call(bf16[16,16,1152]{2,1,0:T(8,128)(2,1)S(1)} %shard_map.55.x_ref), custom_call_target="tpu_custom_call" | custom-call | tf_op jit(solution)/shard_map/pallas_call | solution.py:196
  21.1 2.0 %collective-permute-start.1 = (bf16[256,1152]{1,0:T(8,128)(2,1)S(1)}, bf16[256,1152]{1,0:T(8,128)(2,1)S(1)}, u32[]{:S(2)}, u32[]{:S(2)}) collective-permute-start(bf16[256,1152]{1,0:T(8,128)(2,1)S(1)} %bitcast.10), channel_id=1, source_target_pairs={{2,0},{4,2},{6,4},{8,6},{10,8},{12,10},{14,12},{16,14},{18,16},{20... | collective-permute-start | bytes 1769480 | tf_op jit(solution)/shard_map/ppermute | solution.py:213
  23.1 4.5 %collective-permute-start = (bf16[256,1152]{1,0:T(8,128)(2,1)S(1)}, bf16[256,1152]{1,0:T(8,128)(2,1)S(1)}, u32[]{:S(2)}, u32[]{:S(2)}) collective-permute-start(bf16[256,1152]{1,0:T(8,128)(2,1)S(1)} %bitcast.11), channel_id=1, source_target_pairs={{0,2},{2,4},{4,6},{6,8},{8,10},{10,12},{12,14},{14,16},{16,18},{18... | collective-permute-start | bytes 1769480 | tf_op jit(solution)/shard_map/ppermute | solution.py:212
  27.6 0.0 copy-done.4
  27.6 0.1 copy.6
  27.7 0.1 rev.3
  27.8 0.0 copy-done.3
  27.8 0.3 copy.8
  28.1 0.1 pad.9.clone
  28.1 5.2 %collective-permute-done.1.right_ref = bf16[256,1152]{1,0:T(8,128)(2,1)S(1)} collective-permute-done((bf16[256,1152]{1,0:T(8,128)(2,1)S(1)}, bf16[256,1152]{1,0:T(8,128)(2,1)S(1)}, u32[]{:S(2)}, u32[]{:S(2)}) %collective-permute-start.1) | collective-permute-done | bytes 589856 | tf_op jit(solution)/shard_map/ppermute | solution.py:213
  33.3 1.1 %collective-permute-done.left_ref = bf16[256,1152]{1,0:T(8,128)(2,1)S(1)} collective-permute-done((bf16[256,1152]{1,0:T(8,128)(2,1)S(1)}, bf16[256,1152]{1,0:T(8,128)(2,1)S(1)}, u32[]{:S(2)}, u32[]{:S(2)}) %collective-permute-start) | collective-permute-done | bytes 589856 | tf_op jit(solution)/shard_map/ppermute | solution.py:212
  34.4 0.0 copy-done.1
  34.4 0.0 copy-done.2
  34.4 16.6 %shard_map.57 = bf16[256,1152]{1,0:T(8,128)(2,1)S(1)} custom-call(s32[1,64]{1,0:T(1,128)S(1)} %copy-done.1, s32[1,64]{1,0:T(1,128)S(1)} %copy-done.2, bf16[256,1152]{1,0:T(8,128)(2,1)S(1)} %collective-permute-done.left_ref, bf16[256,1152]{1,0:T(8,128)(2,1)S(1)} %bitcast.12, bf16[256,1152]{1,0:T(8,128)(2,1)S(1)} %collective-permute-done.1.right_ref, ...), custom_call_target="tpu_custom_call" | custom-call | tf_op jit(solution)/shard_map/pallas_call | solution.py:218
  51.0 23.6 %shard_map.58.landed = bf16[16,16,1152]{2,1,0:T(8,128)(2,1)S(1)} custom-call(bf16[16,16,1152]{2,1,0:T(8,128)(2,1)S(1)} %bitcast.13), custom_call_target="tpu_custom_call" | custom-call | tf_op jit(solution)/shard_map/pallas_call | solution.py:196
  74.6 2.7 %shard_map.59 = bf16[4608,64]{1,0:T(8,128)(2,1)} custom-call(bf16[16,16,1152]{2,1,0:T(8,128)(2,1)S(1)} %shard_map.58.landed), custom_call_target="tpu_custom_call" | custom-call | tf_op jit(solution)/shard_map/pallas_call | solution.py:232
  (1 shorter events, 0.0 us)
Async XLA Ops:
  0.0 1.3 %copy-start = (bf16[2,12,12,16,64]{4,3,2,1,0:T(8,128)(2,1)S(1)}, bf16[2,12,12,16,64]{4,3,2,1,0:T(8,128)(2,1)}, u32[]{:S(2)}) copy-start(bf16[2,12,12,16,64]{4,3,2,1,0:T(8,128)(2,1)} %param.5) | copy-start | bytes 1769476
  1.3 26.3 %copy-start.4 = (f32[9,1,64]{2,1,0:T(1,128)S(1)}, f32[9,1,64]{2,1,0:T(1,128)}, u32[]{:S(2)}) copy-start(f32[9,1,64]{2,1,0:T(1,128)} %param.7) | copy-start | bytes 6916
  1.3 26.5 %copy-start.3 = (bf16[12,12,1,64]{3,1,2,0:T(8,128)(2,1)S(1)}, bf16[12,12,1,64]{3,1,2,0:T(8,128)(2,1)}, u32[]{:S(2)}) copy-start(bf16[12,12,1,64]{3,1,2,0:T(8,128)(2,1)} %param.6) | copy-start | bytes 55300
  2.9 31.6 %copy-start.1 = (s32[1,64]{1,0:T(1,128)S(1)}, s32[1,64]{1,0:T(1,128)}, u32[]{:S(2)}) copy-start(s32[1,64]{1,0:T(1,128)} %near_ref.1) | copy-start | bytes 772
  2.9 31.5 %copy-start.2 = (s32[1,64]{1,0:T(1,128)S(1)}, s32[1,64]{1,0:T(1,128)}, u32[]{:S(2)}) copy-start(s32[1,64]{1,0:T(1,128)} %shift_ref.1) | copy-start | bytes 772
  21.1 12.2 %collective-permute-start.1 = (bf16[256,1152]{1,0:T(8,128)(2,1)S(1)}, bf16[256,1152]{1,0:T(8,128)(2,1)S(1)}, u32[]{:S(2)}, u32[]{:S(2)}) collective-permute-start(bf16[256,1152]{1,0:T(8,128)(2,1)S(1)} %bitcast.10), channel_id=1, source_target_pairs={{2,0},{4,2},{6,4},{8,6},{10,8},{12,10},{14,12},{16,14},{18,16},{20... | collective-permute-start | bytes 1769480 | tf_op jit(solution)/shard_map/ppermute | solution.py:213
  23.1 11.4 %collective-permute-start = (bf16[256,1152]{1,0:T(8,128)(2,1)S(1)}, bf16[256,1152]{1,0:T(8,128)(2,1)S(1)}, u32[]{:S(2)}, u32[]{:S(2)}) collective-permute-start(bf16[256,1152]{1,0:T(8,128)(2,1)S(1)} %bitcast.11), channel_id=1, source_target_pairs={{0,2},{2,4},{4,6},{6,8},{8,10},{10,12},{12,14},{14,16},{16,18},{18... | collective-permute-start | bytes 1769480 | tf_op jit(solution)/shard_map/ppermute | solution.py:212
where the time goes:
time: 77.6 us; the launch traced here: 77.4 us
  Pallas kernels  62.7 us (81%)
  starting transfers between devices  6.46 us (8%)
  waiting for transfers between devices  6.29 us (8%)
  local copies, waits for them, and re-layouts  1.82 us (2%)
    pallas_call x2, Pallas kernels, exchanged(): pl.pallas_call(functools.partial(gather_kernel, groups), out_shape=blocks...  41.8 us
    pallas_call x1, Pallas kernels, on_device(): pl.pallas_call(scatter_kernel, out_shape=jax.ShapeDtypeStruct((energies,...  16.6 us
    ppermute x1, waiting for transfers between devices, on_device(): right = lax.ppermute(own, ('energy', 'slab'), [(j, i) for i, j in up])  5.16 us
    ppermute x1, starting transfers between devices, on_device(): left = lax.ppermute(own, ('energy', 'slab'), up)  4.49 us
    pallas_call x1, Pallas kernels, on_device(): pl.pallas_call(functools.partial(unpack_kernel, groups, per_dev), out_sha...  2.74 us
    ppermute x1, starting transfers between devices, on_device(): right = lax.ppermute(own, ('energy', 'slab'), [(j, i) for i, j in up])  1.97 us
    unnamed x12, local copies, waits for them, and re-layouts  1.67 us
    pallas_call x1, Pallas kernels, on_device(): pl.pallas_call(functools.partial(pack_kernel, groups, per_dev), out_shape...  1.59 us
  transfers between devices with their start and end apart: 2, of which 2 were waited for; matrix products, arithmetic and copies ran while one was open for 1% of the time, Pallas kernels for 0%

commit v1 on v0

v1 whole, which is shorter than its diff:
```python
import functools

import jax
import jax.numpy as jnp
from jax import lax
from jax.experimental import pallas as pl
from jax.experimental.pallas import tpu as pltpu
from jax.sharding import PartitionSpec as P

ORB = 12
NBR = 16
BAND = 9
SHIFT = 32
HALO = 4
BLOCK = 2 * ORB * ORB
PAIR = ORB * ORB
REACH = SHIFT + BAND // 2
SPAN = 64
WINDOW = 128

MESH = pl.DeviceIdType.MESH
NT = (((1,), (1,)), ((), ()))


def order(groups, per_dev):
    count = groups * per_dev
    row = lax.broadcasted_iota(jnp.int32, (count, count), 0)
    atom = lax.broadcasted_iota(jnp.int32, (count, count), 1)
    return (atom == (row % groups) * per_dev + row // groups).astype(jnp.bfloat16)


def eye(count):
    row = lax.broadcasted_iota(jnp.int32, (count, count), 0)
    column = lax.broadcasted_iota(jnp.int32, (count, count), 1)
    return (row == column).astype(jnp.bfloat16)


def partner_of(i, step):
    out, bit = 0, 1
    while bit <= step:
        out = out + bit * lax.rem(lax.div(i, bit) + step // bit, 2)
        bit *= 2
    return lax.div(i, bit) * bit + out if step else i


def pack_kernel(groups, per_dev, x_ref, sent, wide, packed):
    local_e = sent.shape[1]
    tiles = wide.shape[0]
    count = x_ref.shape[1]
    lanes = min(count, 128)
    if lanes < 128:
        wide[...] = jnp.zeros_like(wide)
    for j in range(tiles):
        wide[j, :x_ref.shape[0], :lanes] = x_ref[:, j * 128:j * 128 + lanes].astype(jnp.float32)
    pick = order(groups, per_dev)
    for e in range(local_e):
        rows = jnp.concatenate([wide[j, pl.ds(e, BLOCK, stride=local_e), :] for j in range(tiles)], axis=1)
        rows = rows[:, :count].astype(jnp.bfloat16)
        turned = lax.dot_general(pick, rows, NT, preferred_element_type=jnp.float32)
        flat = jnp.concatenate([turned[i * groups:(i + 1) * groups] for i in range(per_dev)], axis=1)
        for j in range(packed.shape[0]):
            packed[j, pl.ds(e, groups, stride=local_e), :] = flat[:, j * 128:(j + 1) * 128]
    for g in range(groups):
        for j in range(packed.shape[0]):
            sent[g, :, j * 128:(j + 1) * 128] = packed[j, g * local_e:(g + 1) * local_e, :].astype(jnp.bfloat16)


def gather_kernel(inner, layers, side, sent, mats_in, weights_in, ints_in, landed, mats, weights, ints,
                  main_send, main_recv, relay_send, relay_recv, table_send, table_recv):
    me, slab = lax.axis_index("energy"), lax.axis_index("slab")
    slabs = lax.axis_size("slab")
    layer, i = lax.div(me, inner), lax.rem(me, inner)
    chunks = sent.shape[0]
    mine = chunks // inner
    slots = mine + 2
    barrier = pltpu.get_barrier_semaphore()
    first, last = i == 0, i == inner - 1
    below, above = layer > 0, layer < layers - 1
    slab_below, slab_above = slab > 0, slab < slabs - 1
    owner, spot = lax.div(me, layers), lax.rem(me, layers)

    def hail(device, row):
        pl.semaphore_signal(barrier, inc=1, device_id=(device, row), device_id_type=MESH)

    for step in range(1, inner):
        hail(layer * inner + partner_of(i, step), slab)

    @pl.when(first & slab_below)
    def _():
        for j in range(inner):
            hail(layer * inner + j, slab - 1)

    @pl.when(last & slab_above)
    def _():
        for j in range(inner):
            hail(layer * inner + j, slab + 1)

    @pl.when(below)
    def _():
        hail(me - inner, slab)

    @pl.when(above)
    def _():
        hail(me + inner, slab)

    for j in range(layers):
        @pl.when(i * layers + j != me)
        def _():
            hail(i * layers + j, slab)

    one = lambda flag: jnp.where(flag, 1, 0)
    pl.semaphore_wait(
        barrier, inner - 1 + one(slab_above) + one(slab_below) + one(above) + one(below) + layers - one(owner == i))

    piece = side + i

    def block(kind, to):
        if kind == 0:
            return sent.at[pl.ds(to * mine, mine)], landed.at[pl.ds(1, mine), piece], slab
        if kind == 1:
            return (sent.at[lax.rem(to * mine - 1 + chunks, chunks)], landed.at[0, piece],
                    slab + one(to == 0))
        return (sent.at[lax.rem(to * mine + mine, chunks)], landed.at[slots - 1, piece],
                slab - one(to == inner - 1))

    def outgoing(kind, step):
        to = partner_of(i, step)
        src, dst, row = block(kind, to)
        return pltpu.make_async_remote_copy(
            src_ref=src, dst_ref=dst, send_sem=main_send.at[kind, step], recv_sem=main_recv.at[kind, step],
            device_id=(layer * inner + to, row), device_id_type=MESH)

    def incoming(kind, step):
        source = partner_of(i, step)
        at = side + source
        dst = (landed.at[pl.ds(1, mine), at], landed.at[0, at], landed.at[slots - 1, at])[kind]
        src = sent.at[pl.ds(0, mine)] if kind == 0 else sent.at[0]
        return pltpu.make_async_remote_copy(
            src_ref=src, dst_ref=dst, send_sem=main_send.at[kind, step], recv_sem=main_recv.at[kind, step],
            device_id=(layer * inner + source, slab), device_id_type=MESH)

    def leaves(kind, step):
        to = partner_of(i, step)
        if kind == 0:
            return None
        if kind == 1:
            return (to > 0) | slab_above
        return (to < inner - 1) | slab_below

    def arrives(kind):
        if kind == 0:
            return None
        if kind == 1:
            return (i > 0) | slab_below
        return (i < inner - 1) | slab_above

    def guarded(flag, act):
        if flag is None:
            act()
        else:
            pl.when(flag)(act)

    for step in range(1, inner):
        for kind in range(3):
            guarded(leaves(kind, step), lambda: outgoing(kind, step).start())

    @pl.when(first & slab_above)
    def _():
        outgoing(1, 0).start()

    @pl.when(last & slab_below)
    def _():
        outgoing(2, 0).start()

    landed[pl.ds(1, mine), piece] = sent[pl.ds(i * mine, mine)]

    @pl.when(i > 0)
    def _():
        landed[0, piece] = sent[lax.rem(i * mine - 1 + chunks, chunks)]

    @pl.when(i < inner - 1)
    def _():
        landed[slots - 1, piece] = sent[lax.rem(i * mine + mine, chunks)]

    @pl.when(first & jnp.logical_not(slab_below))
    def _():
        landed[0, side:side + inner] = jnp.zeros((inner,) + landed.shape[2:], landed.dtype)

    @pl.when(last & jnp.logical_not(slab_above))
    def _():
        landed[slots - 1, side:side + inner] = jnp.zeros((inner,) + landed.shape[2:], landed.dtype)

    tables = ((mats_in, mats), (weights_in, weights), (ints_in, ints))

    def table(number, j, to):
        src, dst = tables[number]
        return pltpu.make_async_remote_copy(
            src_ref=src, dst_ref=dst.at[j], send_sem=table_send.at[number, 0], recv_sem=table_recv.at[number, 0],
            device_id=(to, slab), device_id_type=MESH)

    for j in range(layers):
        to = j * inner + owner

        @pl.when(to != me)
        def _():
            for number in range(3):
                src, dst = tables[number]
                pltpu.make_async_remote_copy(
                    src_ref=src, dst_ref=dst.at[spot], send_sem=table_send.at[number, j],
                    recv_sem=table_recv.at[number, spot], device_id=(to, slab), device_id_type=MESH).start()

    @pl.when(owner == i)
    def _():
        for src, dst in tables:
            dst[spot] = src[...]

    def relay(way, source):
        at = source - (inner - side) if way == 0 else source
        into = at if way == 0 else side + inner + source
        return pltpu.make_async_remote_copy(
            src_ref=landed.at[:, side + source], dst_ref=landed.at[:, into],
            send_sem=relay_send.at[way, at], recv_sem=relay_recv.at[way, at],
            device_id=(me + inner if way == 0 else me - inner, slab), device_id_type=MESH)

    for step in range(inner):
        source = partner_of(i, step)
        for kind in range(3):
            if step:
                guarded(arrives(kind), lambda: incoming(kind, step).wait_recv())
        if step == 0:
            pl.when(first & slab_below)(lambda: incoming(1, 0).wait_recv())
            pl.when(last & slab_above)(lambda: incoming(2, 0).wait_recv())
        pl.when(above & (source >= inner - side))(lambda: relay(0, source).start())
        pl.when(below & (source < side))(lambda: relay(1, source).start())

    def zero(start):
        landed[:, start:start + side] = jnp.zeros((slots, side) + landed.shape[2:], landed.dtype)

    pl.when(jnp.logical_not(below))(lambda: zero(0))
    pl.when(jnp.logical_not(above))(lambda: zero(side + inner))

    def relayed(way, at):
        into = at if way == 0 else side + inner + at
        return pltpu.make_async_remote_copy(
            src_ref=landed.at[:, into], dst_ref=landed.at[:, into],
            send_sem=relay_send.at[way, at], recv_sem=relay_recv.at[way, at],
            device_id=(me - inner if way == 0 else me + inner, slab), device_id_type=MESH)

    for at in range(side):
        pl.when(below)(lambda: relayed(0, at).wait_recv())
        pl.when(above)(lambda: relayed(1, at).wait_recv())

    for j in range(layers):
        @pl.when(i * layers + j != me)
        def _():
            for number in range(3):
                src, dst = tables[number]
                pltpu.make_async_remote_copy(
                    src_ref=src, dst_ref=dst.at[j], send_sem=table_send.at[number, j],
                    recv_sem=table_recv.at[number, j], device_id=(me, slab), device_id_type=MESH).wait_recv()

        @pl.when(j * inner + owner != me)
        def _():
            for number in range(3):
                src, dst = tables[number]
                pltpu.make_async_remote_copy(
                    src_ref=src, dst_ref=dst.at[j], send_sem=table_send.at[number, j],
                    recv_sem=table_recv.at[number, j], device_id=(me, slab), device_id_type=MESH).wait_send()

    for step in range(1, inner):
        for kind in range(3):
            guarded(leaves(kind, step), lambda: outgoing(kind, step).wait_send())
    pl.when(first & slab_above)(lambda: outgoing(1, 0).wait_send())
    pl.when(last & slab_below)(lambda: outgoing(2, 0).wait_send())
    for at in range(side):
        pl.when(above)(lambda: relayed(0, at).wait_send())
        pl.when(below)(lambda: relayed(1, at).wait_send())


def back_kernel(inner, out_ref, landed, send_sem, recv_sem):
    me, slab = lax.axis_index("energy"), lax.axis_index("slab")
    layer, i = lax.div(me, inner), lax.rem(me, inner)
    mine = out_ref.shape[1]
    barrier = pltpu.get_barrier_semaphore()
    for step in range(1, inner):
        pl.semaphore_signal(
            barrier, inc=1, device_id=(layer * inner + partner_of(i, step), slab), device_id_type=MESH)
    pl.semaphore_wait(barrier, inner - 1)

    def copy(step, at):
        to = partner_of(i, step)
        return pltpu.make_async_remote_copy(
            src_ref=out_ref.at[to], dst_ref=landed.at[pl.ds(at * mine, mine)],
            send_sem=send_sem.at[step], recv_sem=recv_sem.at[step],
            device_id=(layer * inner + to, slab), device_id_type=MESH)

    for step in range(1, inner):
        copy(step, i).start()
    landed[pl.ds(i * mine, mine)] = out_ref[i]
    for step in range(1, inner):
        copy(step, partner_of(i, step)).wait_recv()
        copy(step, i).wait_send()


def unpack_kernel(groups, per_dev, landed, out_ref, wide, tall):
    local_e = landed.shape[1]
    lanes = min(out_ref.shape[1], 128)
    for g in range(groups):
        for j in range(wide.shape[0]):
            wide[j, g * local_e:(g + 1) * local_e, :] = landed[g, :, j * 128:(j + 1) * 128].astype(jnp.float32)
    pick = order(groups, per_dev)
    for e in range(local_e):
        rows = jnp.concatenate(
            [wide[j, pl.ds(e, groups, stride=local_e), :] for j in range(wide.shape[0])], axis=1)
        stack = jnp.concatenate([rows[:, i * BLOCK:(i + 1) * BLOCK] for i in range(per_dev)], axis=0)
        turned = jnp.dot(stack.T.astype(jnp.bfloat16), pick, preferred_element_type=jnp.float32)
        if lanes < 128:
            turned = jnp.concatenate([turned, jnp.zeros((BLOCK, 128 - lanes), jnp.float32)], axis=1)
        for j in range(tall.shape[0]):
            tall[j, pl.ds(e, BLOCK, stride=local_e), :] = turned[:, j * 128:(j + 1) * 128]
    for j in range(tall.shape[0]):
        out_ref[:, j * 128:j * 128 + lanes] = tall[j, :out_ref.shape[0], :lanes].astype(jnp.bfloat16)


def scatter_kernel(side, ints_ref, landed, weight_ref, matrix_ref, out_ref,
                   green, spread_q, spread_r, both, bands, stage):
    slots, pieces, local_e, width = landed.shape
    inner = pieces - 2 * side
    mine = slots - 2
    rows_e = pieces * local_e
    late = rows_e - WINDOW
    slab_atoms = inner * mine * HALO
    first_atom = (lax.axis_index("slab") * slab_atoms
                  + lax.rem(lax.axis_index("energy"), inner) * mine * HALO - HALO)
    unit = eye(128)

    def turn(slot, carry):
        if local_e % 16:
            for piece in range(pieces):
                stage[piece * local_e:(piece + 1) * local_e, :] = landed[slot, piece].astype(jnp.float32)
            tall = stage[...].astype(jnp.bfloat16)
        else:
            tall = landed[slot].reshape(rows_e, width)
        two = jnp.concatenate([tall[:WINDOW], tall[late:]], axis=0)
        turned = jnp.concatenate([
            lax.dot_general(unit, two[:, j * 128:(j + 1) * 128], NT, preferred_element_type=jnp.float32).astype(
                jnp.bfloat16) for j in range(width // 128)], axis=0)
        for atom in range(HALO):
            for c in range(2):
                start = (2 * atom + c) * PAIR
                for window in range(2):
                    green[window, slot * HALO + atom, :, c * WINDOW:(c + 1) * WINDOW] = (
                        turned[start:start + PAIR, window * WINDOW:(window + 1) * WINDOW])
        return carry

    lax.fori_loop(0, slots, turn, 0)

    wide = NBR * PAIR
    lane = lax.broadcasted_iota(jnp.int32, (8, wide), 1)
    key_q = (lane // ORB)[:1]
    key_r = (lane // PAIR * ORB + lane % ORB)[:1]
    row = lax.broadcasted_iota(jnp.int32, (NBR * ORB, wide), 0)
    count = matrix_ref.shape[0] * matrix_ref.shape[1]
    matrices = matrix_ref[...].reshape(count, matrix_ref.shape[2])[:, :NBR * ORB]
    spread_q[...] = jnp.dot(matrices, (row == key_q).astype(jnp.bfloat16), preferred_element_type=jnp.float32)
    spread_r[...] = jnp.dot(matrices, (row == key_r).astype(jnp.bfloat16), preferred_element_type=jnp.float32)

    sub = lax.broadcasted_iota(jnp.int32, (8, WINDOW), 0)
    left_half = lax.broadcasted_iota(jnp.int32, (WINDOW, WINDOW), 1) < SPAN
    low_rows = lax.broadcasted_iota(jnp.int32, (8, wide), 0) < 4

    def chunk(m, carry):
        parts = []
        for a in range(HALO):
            atom = m * HALO + a
            for k in range(NBR):
                index = a * NBR + k
                shift = ints_ref[m, 1, index]
                later = jnp.where(shift >= 0, 1, 0)
                base = shift + side * local_e - BAND // 2 - later * late
                weight = weight_ref[m, pl.ds(index, 1), :]
                tile = pltpu.roll(jnp.broadcast_to(weight, (8, WINDOW)), WINDOW - BAND + 1 - base, 1)
                for step in (1, 2, 4):
                    tile = jnp.where((sub & step) != 0, pltpu.roll(tile, step, 1), tile)
                tiles = [tile] + [pltpu.roll(tile, 8 * b, 1) for b in range(1, WINDOW // 8)]
                band = jnp.concatenate(tiles, axis=0)
                turned_band = jnp.concatenate(tiles[SPAN // 8:] + tiles[:SPAN // 8], axis=0)
                toeplitz = jnp.concatenate([
                    jnp.where(left_half, band, 0.0).astype(jnp.bfloat16),
                    jnp.where(left_half, 0.0, turned_band).astype(jnp.bfloat16)], axis=0)
                partner = jnp.clip(ints_ref[m, 0, index] - first_atom, 0, slots * HALO - 1)
                banded = jnp.dot(green[later, partner], toeplitz, preferred_element_type=jnp.float32)
                bands[a % 2, k * PAIR:(k + 1) * PAIR, :] = banded.astype(jnp.bfloat16)
            right = spread_r[pl.ds(pl.multiple_of(atom * 16, 16), 16), :]
            rights = (right[:8], jnp.concatenate([right[8:12], right[:4]], axis=0), right[4:12])
            for four in range(ORB // 4):
                rows = []
                for h in range(2):
                    p = four * 4 + h * 2
                    q0 = spread_q[pl.ds(atom * 16 + p, 1), :]
                    q1 = spread_q[pl.ds(atom * 16 + p + 1, 1), :]
                    rows += [q0 * rights[0], jnp.where(low_rows, q0, q1) * rights[1], q1 * rights[2]]
                both[a % 2, four * 48:(four + 1) * 48, :] = jnp.concatenate(rows, axis=0).astype(jnp.bfloat16)
            total = jnp.dot(both[a % 2], bands[a % 2], preferred_element_type=jnp.float32)
            turned = lax.dot_general(unit, total.astype(jnp.bfloat16), NT, preferred_element_type=jnp.float32)
            parts += [turned[:SPAN], turned[SPAN:]]
        whole = jnp.concatenate(parts, axis=1)
        for d in range(inner):
            out_ref[d, m] = whole[d * local_e:(d + 1) * local_e].astype(jnp.bfloat16)
        return carry

    lax.fori_loop(0, mine, chunk, 0)


def on_device(green_blocks, couplings, band_weights, neighbours, shifts):
    groups = lax.axis_size("energy")
    local_e, slab_count = green_blocks.shape[3:]
    per_dev = slab_count // groups
    width = per_dev * BLOCK
    pairs = per_dev * NBR
    inner = SPAN // local_e
    layers = groups // inner
    side = pl.cdiv(REACH, local_e)
    pieces = inner + 2 * side
    mine = groups // inner
    slots = mine + 2
    assert per_dev == HALO and side <= inner and pieces * local_e >= WINDOW
    vmem = pl.BlockSpec(memory_space=pltpu.VMEM)
    smem = pl.BlockSpec(memory_space=pltpu.SMEM)
    blocks = jax.ShapeDtypeStruct((groups, local_e, width), jnp.bfloat16)
    wide = pltpu.VMEM((pl.cdiv(slab_count, 128), BLOCK * local_e, 128), jnp.float32)
    packed = pltpu.VMEM((width // 128, local_e * groups, 128), jnp.float32)
    room = pltpu.CompilerParams(vmem_limit_bytes=32 * 1024 * 1024)

    matrix = couplings.reshape(ORB, ORB, per_dev, NBR).transpose(2, 0, 3, 1).reshape(per_dev, ORB, NBR * ORB)
    matrix = jnp.pad(matrix, ((0, 0), (0, 16 - ORB), (0, 256 - NBR * ORB))).reshape(per_dev * 16, 256)
    weight = jnp.pad(band_weights.reshape(BAND, pairs)[::-1].T, ((0, 0), (0, WINDOW - BAND)))
    ints = jnp.pad(jnp.concatenate([neighbours, shifts], axis=0), ((0, 6), (0, 128 - pairs)))

    sent = pl.pallas_call(
        functools.partial(pack_kernel, groups, per_dev),
        out_shape=blocks, in_specs=[vmem], out_specs=vmem,
        scratch_shapes=[wide, packed], compiler_params=room,
    )(green_blocks.reshape(BLOCK * local_e, slab_count))

    landed, mats, weights, numbers = pl.pallas_call(
        functools.partial(gather_kernel, inner, layers, side),
        out_shape=(
            jax.ShapeDtypeStruct((slots, pieces, local_e, width), jnp.bfloat16),
            jax.ShapeDtypeStruct((layers,) + matrix.shape, jnp.bfloat16),
            jax.ShapeDtypeStruct((layers,) + weight.shape, jnp.float32),
            jax.ShapeDtypeStruct((layers,) + ints.shape, jnp.int32),
        ),
        in_specs=[vmem] * 4, out_specs=(vmem,) * 4,
        scratch_shapes=[
            pltpu.SemaphoreType.DMA((3, inner)), pltpu.SemaphoreType.DMA((3, inner)),
            pltpu.SemaphoreType.DMA((2, side)), pltpu.SemaphoreType.DMA((2, side)),
            pltpu.SemaphoreType.DMA((3, layers)), pltpu.SemaphoreType.DMA((3, layers)),
        ],
        compiler_params=pltpu.CompilerParams(
            collective_id=0, has_side_effects=True, vmem_limit_bytes=32 * 1024 * 1024),
    )(sent, matrix, weight, ints)

    out = pl.pallas_call(
        functools.partial(scatter_kernel, side),
        out_shape=jax.ShapeDtypeStruct((inner, mine, local_e, width), jnp.bfloat16),
        in_specs=[smem, vmem, vmem, vmem],
        out_specs=vmem,
        scratch_shapes=[
            pltpu.VMEM((2, slots * HALO, PAIR, 2 * WINDOW), jnp.bfloat16),
            pltpu.VMEM((mine * HALO * 16, NBR * PAIR), jnp.float32),
            pltpu.VMEM((mine * HALO * 16, NBR * PAIR), jnp.float32),
            pltpu.VMEM((2, PAIR, NBR * PAIR), jnp.bfloat16),
            pltpu.VMEM((2, NBR * PAIR, WINDOW), jnp.bfloat16),
            pltpu.VMEM((pieces * local_e, width), jnp.float32),
        ],
        compiler_params=pltpu.CompilerParams(vmem_limit_bytes=40 * 1024 * 1024),
    )(numbers, landed, weights, mats)

    back = pl.pallas_call(
        functools.partial(back_kernel, inner),
        out_shape=blocks, in_specs=[vmem], out_specs=vmem,
        scratch_shapes=[pltpu.SemaphoreType.DMA((inner,)), pltpu.SemaphoreType.DMA((inner,))],
        compiler_params=pltpu.CompilerParams(
            collective_id=1, has_side_effects=True, vmem_limit_bytes=32 * 1024 * 1024),
    )(out)
    result = pl.pallas_call(
        functools.partial(unpack_kernel, groups, per_dev),
        out_shape=jax.ShapeDtypeStruct((BLOCK * local_e, slab_count), jnp.bfloat16),
        in_specs=[vmem], out_specs=vmem,
        scratch_shapes=[packed, wide], compiler_params=room,
    )(back)
    return result.reshape(2, ORB, ORB, local_e, slab_count)


def solution(mesh):
    return jax.shard_map(
        on_device,
        mesh=mesh,
        in_specs=(
            P(None, None, None, "energy", "slab"),
            P(None, None, "slab", "energy"),
            P(None, "slab", "energy"),
            P("slab", "energy"),
            P("slab", "energy"),
        ),
        out_specs=P(None, None, None, "energy", "slab"),
        check_vma=False,
    )
```

time: 77.6 us -> 66.3 us (0.85)
  the two profiles are of different devices: /device:TPU:15 before, /device:TPU:0 now
where the time goes in v1:
time: 66.3 us; the launch traced here: 65 us
  Pallas kernels  60.9 us (92%)
  local copies, waits for them, and re-layouts  3.34 us (5%)
  other arithmetic  0.68 us (1%)
    pallas_call x1, Pallas kernels, on_device(): pl.pallas_call(functools.partial(gather_kernel, inner, layers, side), out...  25.5 us
    pallas_call x1, Pallas kernels, on_device(): pl.pallas_call(functools.partial(scatter_kernel, side), out_shape=jax.Sha...  22.1 us
    pallas_call x1, Pallas kernels, on_device(): pl.pallas_call(functools.partial(back_kernel, inner), out_shape=blocks, i...  8.99 us
    pallas_call x1, Pallas kernels, on_device(): pl.pallas_call(functools.partial(unpack_kernel, groups, per_dev), out_sha...  2.74 us
    unnamed x4, local copies, waits for them, and re-layouts  2.05 us
    pallas_call x1, Pallas kernels, on_device(): pl.pallas_call(functools.partial(pack_kernel, groups, per_dev), out_shape...  1.59 us

profile of v1, /device:TPU:0, one launch (start us, length us, event | category | flops | bytes accessed | tf_op | source)
XLA Modules:
  0.0 65.0 jit_solution(15560677485159153968)
XLA Ops:
  0.0 0.7 %pad_add_fusion = s32[2,64]{1,0:T(2,128)S(1)} fusion(s32[1,64]{1,0:T(1,128)} %param.9, s32[1,64]{1,0:T(1,128)} %param.8), kind=kLoop, calls=%fused_computation | loop fusion | flops 128 | bytes 1024 | tf_op jit(solution)/shard_map/concatenate | solution.py:438
  0.7 0.8 %copy.10 = f32[9,1,64]{0,2,1:T(8,128)S(1)} copy(f32[9,1,64]{2,1,0:T(1,128)} %param.7) | data formatting | bytes 4608 | tf_op args[2]
  1.5 0.1 rev.3
  1.6 1.0 %copy.11 = bf16[12,12,1,64]{1,3,0,2:T(8,128)(2,1)S(1)} copy(bf16[12,12,1,64]{3,1,2,0:T(8,128)(2,1)} %param.6) | data formatting | bytes 36864 | tf_op jit(solution)/shard_map/reshape | solution.py:435
  2.5 0.2 reshape.20
  2.8 0.0 copy-start
  2.8 1.3 %copy-done = bf16[2,12,12,16,64]{4,3,2,1,0:T(8,128)(2,1)S(1)} copy-done((bf16[2,12,12,16,64]{4,3,2,1,0:T(8,128)(2,1)S(1)}, bf16[2,12,12,16,64]{4,3,2,1,0:T(8,128)(2,1)}, u32[]{:S(2)}) %copy-start) | copy-done | bytes 589848
  4.1 1.6 %shard_map.55.sent = bf16[16,16,1152]{2,1,0:T(8,128)(2,1)S(1)} custom-call(bf16[4608,64]{1,0:T(8,128)(2,1)S(1)} %bitcast.12), custom_call_target="tpu_custom_call" | custom-call | tf_op jit(solution)/shard_map/pallas_call | solution.py:440
  5.7 25.5 %shard_map.56 = (bf16[6,10,16,1152]{3,2,1,0:T(8,128)(2,1)S(1)}, bf16[4,64,256]{2,1,0:T(8,128)(2,1)S(1)}, f32[4,64,128]{2,1,0:T(8,128)S(1)}, s32[4,8,128]{2,1,0:T(8,128)S(1)}) custom-call(bf16[16,16,1152]{2,1,0:T(8,128)(2,1)S(1)} %shard_map.55.sent, bf16[64,256]{1,0:T(8,128)(2,1)S(1)} %bitcast.13, f32[64,128]{1,0:T(8,128)S(1)} %pad.13.weights_in, ...), custom_call_target="tpu_custom_call" | custom-call | tf_op jit(solution)/shard_map/pallas_call | solution.py:446
  31.2 22.1 %shard_map.57.out_ref = bf16[4,4,16,1152]{3,2,1,0:T(8,128)(2,1)S(1)} custom-call(s32[4,8,128]{2,1,0:T(8,128)S(1)} %get-tuple-element.9.ints_ref, bf16[6,10,16,1152]{3,2,1,0:T(8,128)(2,1)S(1)} %get-tuple-element.10.landed, f32[4,64,128]{2,1,0:T(8,128)S(1)} %get-tuple-element.11.weight_ref, bf16[4,64,256]{2,1,0:T(8,128)(2,1)S(1)} %get-tuple-element.12.matrix_ref), custom_call_target="tpu_custom_call" | custom-call | tf_op jit(solution)/shard_map/pallas_call | solution.py:464
  53.3 9.0 %shard_map.58.landed = bf16[16,16,1152]{2,1,0:T(8,128)(2,1)S(1)} custom-call(bf16[4,4,16,1152]{3,2,1,0:T(8,128)(2,1)S(1)} %shard_map.57.out_ref), custom_call_target="tpu_custom_call" | custom-call | tf_op jit(solution)/shard_map/pallas_call | solution.py:480
  62.3 2.7 %shard_map.59 = bf16[4608,64]{1,0:T(8,128)(2,1)} custom-call(bf16[16,16,1152]{2,1,0:T(8,128)(2,1)S(1)} %shard_map.58.landed), custom_call_target="tpu_custom_call" | custom-call | tf_op jit(solution)/shard_map/pallas_call | solution.py:487
  (4 shorter events, 0.0 us)
Async XLA Ops:
  2.8 1.3 %copy-start = (bf16[2,12,12,16,64]{4,3,2,1,0:T(8,128)(2,1)S(1)}, bf16[2,12,12,16,64]{4,3,2,1,0:T(8,128)(2,1)}, u32[]{:S(2)}) copy-start(bf16[2,12,12,16,64]{4,3,2,1,0:T(8,128)(2,1)} %param.5) | copy-start | bytes 1769476

commit v2 on v1

--- a/solution.py
+++ b/solution.py
@@ -277,31 +277,6 @@
         pl.when(below)(lambda: relayed(1, at).wait_send())
 
 
-def back_kernel(inner, out_ref, landed, send_sem, recv_sem):
-    me, slab = lax.axis_index("energy"), lax.axis_index("slab")
-    layer, i = lax.div(me, inner), lax.rem(me, inner)
-    mine = out_ref.shape[1]
-    barrier = pltpu.get_barrier_semaphore()
-    for step in range(1, inner):
-        pl.semaphore_signal(
-            barrier, inc=1, device_id=(layer * inner + partner_of(i, step), slab), device_id_type=MESH)
-    pl.semaphore_wait(barrier, inner - 1)
-
-    def copy(step, at):
-        to = partner_of(i, step)
-        return pltpu.make_async_remote_copy(
-            src_ref=out_ref.at[to], dst_ref=landed.at[pl.ds(at * mine, mine)],
-            send_sem=send_sem.at[step], recv_sem=recv_sem.at[step],
-            device_id=(layer * inner + to, slab), device_id_type=MESH)
-
-    for step in range(1, inner):
-        copy(step, i).start()
-    landed[pl.ds(i * mine, mine)] = out_ref[i]
-    for step in range(1, inner):
-        copy(step, partner_of(i, step)).wait_recv()
-        copy(step, i).wait_send()
-
-
 def unpack_kernel(groups, per_dev, landed, out_ref, wide, tall):
     local_e = landed.shape[1]
     lanes = min(out_ref.shape[1], 128)
@@ -322,8 +297,8 @@
         out_ref[:, j * 128:j * 128 + lanes] = tall[j, :out_ref.shape[0], :lanes].astype(jnp.bfloat16)
 
 
-def scatter_kernel(side, ints_ref, landed, weight_ref, matrix_ref, out_ref,
-                   green, spread_q, spread_r, both, bands, stage):
+def scatter_kernel(side, ints_ref, landed, weight_ref, matrix_ref, back_ref,
+                   out_ref, green, spread_q, spread_r, both, bands, stage, send_sem, recv_sem):
     slots, pieces, local_e, width = landed.shape
     inner = pieces - 2 * side
     mine = slots - 2
@@ -333,6 +308,20 @@
     first_atom = (lax.axis_index("slab") * slab_atoms
                   + lax.rem(lax.axis_index("energy"), inner) * mine * HALO - HALO)
     unit = eye(128)
+    me, slab = lax.axis_index("energy"), lax.axis_index("slab")
+    base_of_layer, i = lax.div(me, inner) * inner, lax.rem(me, inner)
+    barrier = pltpu.get_barrier_semaphore()
+    for step in range(1, inner):
+        pl.semaphore_signal(
+            barrier, inc=1, device_id=(base_of_layer + partner_of(i, step), slab), device_id_type=MESH)
+    pl.semaphore_wait(barrier, inner - 1)
+
+    def share(step, m, owner):
+        to = partner_of(i, step)
+        return pltpu.make_async_remote_copy(
+            src_ref=out_ref.at[to, m], dst_ref=back_ref.at[owner * mine + m],
+            send_sem=send_sem.at[step, m], recv_sem=recv_sem.at[step, m],
+            device_id=(base_of_layer + to, slab), device_id_type=MESH)
 
     def turn(slot, carry):
         if local_e % 16:
@@ -407,9 +396,20 @@
         whole = jnp.concatenate(parts, axis=1)
         for d in range(inner):
             out_ref[d, m] = whole[d * local_e:(d + 1) * local_e].astype(jnp.bfloat16)
+        for step in range(1, inner):
+            share(step, m, i).start()
+        back_ref[i * mine + m] = out_ref[i, m]
         return carry
 
     lax.fori_loop(0, mine, chunk, 0)
+
+    def finish(m, carry):
+        for step in range(1, inner):
+            share(step, m, partner_of(i, step)).wait_recv()
+            share(step, m, i).wait_send()
+        return carry
+
+    lax.fori_loop(0, mine, finish, 0)
 
 
 def on_device(green_blocks, couplings, band_weights, neighbours, shifts):
@@ -461,29 +461,24 @@
             collective_id=0, has_side_effects=True, vmem_limit_bytes=32 * 1024 * 1024),
     )(sent, matrix, weight, ints)
 
-    out = pl.pallas_call(
+    back = pl.pallas_call(
         functools.partial(scatter_kernel, side),
-        out_shape=jax.ShapeDtypeStruct((inner, mine, local_e, width), jnp.bfloat16),
+        out_shape=blocks,
         in_specs=[smem, vmem, vmem, vmem],
         out_specs=vmem,
         scratch_shapes=[
+            pltpu.VMEM((inner, mine, local_e, width), jnp.bfloat16),
             pltpu.VMEM((2, slots * HALO, PAIR, 2 * WINDOW), jnp.bfloat16),
             pltpu.VMEM((mine * HALO * 16, NBR * PAIR), jnp.float32),
             pltpu.VMEM((mine * HALO * 16, NBR * PAIR), jnp.float32),
             pltpu.VMEM((2, PAIR, NBR * PAIR), jnp.bfloat16),
             pltpu.VMEM((2, NBR * PAIR, WINDOW), jnp.bfloat16),
             pltpu.VMEM((pieces * local_e, width), jnp.float32),
+            pltpu.SemaphoreType.DMA((inner, mine)), pltpu.SemaphoreType.DMA((inner, mine)),
         ],
-        compiler_params=pltpu.CompilerParams(vmem_limit_bytes=40 * 1024 * 1024),
+        compiler_params=pltpu.CompilerParams(
+            collective_id=1, has_side_effects=True, vmem_limit_bytes=40 * 1024 * 1024),
     )(numbers, landed, weights, mats)
-
-    back = pl.pallas_call(
-        functools.partial(back_kernel, inner),
-        out_shape=blocks, in_specs=[vmem], out_specs=vmem,
-        scratch_shapes=[pltpu.SemaphoreType.DMA((inner,)), pltpu.SemaphoreType.DMA((inner,))],
-        compiler_params=pltpu.CompilerParams(
-            collective_id=1, has_side_effects=True, vmem_limit_bytes=32 * 1024 * 1024),
-    )(out)
     result = pl.pallas_call(
         functools.partial(unpack_kernel, groups, per_dev),
         out_shape=jax.ShapeDtypeStruct((BLOCK * local_e, slab_count), jnp.bfloat16),

time: 66.3 us -> 61.7 us (0.931)
  Pallas kernels: 60.9 us -> 56.4 us
    pallas_call x2 -> x1, Pallas kernels: 31.1 us -> 26.6 us  [on_device(): pl.pallas_call(functools.partial(scatter_kernel, side), out_shape=blocks,...]
where the time goes in v2:
time: 61.7 us; the launch traced here: 60.5 us
  Pallas kernels  56.4 us (91%)
  local copies, waits for them, and re-layouts  3.34 us (5%)
  other arithmetic  0.68 us (1%)
    pallas_call x1, Pallas kernels, on_device(): pl.pallas_call(functools.partial(scatter_kernel, side), out_shape=blocks,...  26.6 us
    pallas_call x1, Pallas kernels, on_device(): pl.pallas_call(functools.partial(gather_kernel, inner, layers, side), out...  25.5 us
    pallas_call x1, Pallas kernels, on_device(): pl.pallas_call(functools.partial(unpack_kernel, groups, per_dev), out_sha...  2.74 us
    unnamed x4, local copies, waits for them, and re-layouts  2.05 us
    pallas_call x1, Pallas kernels, on_device(): pl.pallas_call(functools.partial(pack_kernel, groups, per_dev), out_shape...  1.59 us

profile of v2, /device:TPU:0, one launch (start us, length us, event | category | flops | bytes accessed | tf_op | source)
XLA Modules:
  0.0 60.5 jit_solution(6274547923816161199)
XLA Ops:
  0.0 0.7 %pad_add_fusion = s32[2,64]{1,0:T(2,128)S(1)} fusion(s32[1,64]{1,0:T(1,128)} %param.9, s32[1,64]{1,0:T(1,128)} %param.8), kind=kLoop, calls=%fused_computation | loop fusion | flops 128 | bytes 1024 | tf_op jit(solution)/shard_map/concatenate | solution.py:438
  0.7 0.8 %copy.10 = f32[9,1,64]{0,2,1:T(8,128)S(1)} copy(f32[9,1,64]{2,1,0:T(1,128)} %param.7) | data formatting | bytes 4608 | tf_op args[2]
  1.5 0.1 rev.3
  1.6 1.0 %copy.11 = bf16[12,12,1,64]{1,3,0,2:T(8,128)(2,1)S(1)} copy(bf16[12,12,1,64]{3,1,2,0:T(8,128)(2,1)} %param.6) | data formatting | bytes 36864 | tf_op jit(solution)/shard_map/reshape | solution.py:435
  2.5 0.2 reshape.20
  2.8 0.0 copy-start
  2.8 1.3 %copy-done = bf16[2,12,12,16,64]{4,3,2,1,0:T(8,128)(2,1)S(1)} copy-done((bf16[2,12,12,16,64]{4,3,2,1,0:T(8,128)(2,1)S(1)}, bf16[2,12,12,16,64]{4,3,2,1,0:T(8,128)(2,1)}, u32[]{:S(2)}) %copy-start) | copy-done | bytes 589848
  4.1 1.6 %shard_map.55.sent = bf16[16,16,1152]{2,1,0:T(8,128)(2,1)S(1)} custom-call(bf16[4608,64]{1,0:T(8,128)(2,1)S(1)} %bitcast.12), custom_call_target="tpu_custom_call" | custom-call | tf_op jit(solution)/shard_map/pallas_call | solution.py:440
  5.7 25.5 %shard_map.56 = (bf16[6,10,16,1152]{3,2,1,0:T(8,128)(2,1)S(1)}, bf16[4,64,256]{2,1,0:T(8,128)(2,1)S(1)}, f32[4,64,128]{2,1,0:T(8,128)S(1)}, s32[4,8,128]{2,1,0:T(8,128)S(1)}) custom-call(bf16[16,16,1152]{2,1,0:T(8,128)(2,1)S(1)} %shard_map.55.sent, bf16[64,256]{1,0:T(8,128)(2,1)S(1)} %bitcast.13, f32[64,128]{1,0:T(8,128)S(1)} %pad.13.weights_in, ...), custom_call_target="tpu_custom_call" | custom-call | tf_op jit(solution)/shard_map/pallas_call | solution.py:446
  31.2 26.6 %shard_map.57.landed = bf16[16,16,1152]{2,1,0:T(8,128)(2,1)S(1)} custom-call(s32[4,8,128]{2,1,0:T(8,128)S(1)} %get-tuple-element.9.ints_ref, bf16[6,10,16,1152]{3,2,1,0:T(8,128)(2,1)S(1)} %get-tuple-element.10.landed, f32[4,64,128]{2,1,0:T(8,128)S(1)} %get-tuple-element.11.weight_ref, bf16[4,64,256]{2,1,0:T(8,128)(2,1)S(1)} %get-tuple-element.12.matrix_ref), custom_call_target="tpu_custom_call" | custom-call | tf_op jit(solution)/shard_map/pallas_call | solution.py:464
  57.8 2.7 %shard_map.58 = bf16[4608,64]{1,0:T(8,128)(2,1)} custom-call(bf16[16,16,1152]{2,1,0:T(8,128)(2,1)S(1)} %shard_map.57.landed), custom_call_target="tpu_custom_call" | custom-call | tf_op jit(solution)/shard_map/pallas_call | solution.py:482
  (4 shorter events, 0.0 us)
Async XLA Ops:
  2.8 1.3 %copy-start = (bf16[2,12,12,16,64]{4,3,2,1,0:T(8,128)(2,1)S(1)}, bf16[2,12,12,16,64]{4,3,2,1,0:T(8,128)(2,1)}, u32[]{:S(2)}) copy-start(bf16[2,12,12,16,64]{4,3,2,1,0:T(8,128)(2,1)} %param.5) | copy-start | bytes 1769476

commit v3 on v0

v3 whole, which is shorter than its diff:
```python
import functools

import jax
import jax.numpy as jnp
from jax import lax
from jax.experimental import pallas as pl
from jax.experimental.pallas import tpu as pltpu
from jax.sharding import PartitionSpec as P

ORB = 12
NBR = 16
BAND = 9
SHIFT = 32
HALO = 4
BLOCK = 2 * ORB * ORB
PAIR = ORB * ORB
REACH = SHIFT + BAND // 2
SPAN = 64
WINDOW = 128

MESH = pl.DeviceIdType.MESH
NT = (((1,), (1,)), ((), ()))


def order(groups, per_dev):
    count = groups * per_dev
    row = lax.broadcasted_iota(jnp.int32, (count, count), 0)
    atom = lax.broadcasted_iota(jnp.int32, (count, count), 1)
    return (atom == (row % groups) * per_dev + row // groups).astype(jnp.bfloat16)


def eye(count):
    row = lax.broadcasted_iota(jnp.int32, (count, count), 0)
    column = lax.broadcasted_iota(jnp.int32, (count, count), 1)
    return (row == column).astype(jnp.bfloat16)


def partner_of(i, step):
    out, bit = 0, 1
    while bit <= step:
        out = out + bit * lax.rem(lax.div(i, bit) + step // bit, 2)
        bit *= 2
    return lax.div(i, bit) * bit + out if step else i


def pack_kernel(groups, per_dev, x_ref, sent, wide, packed):
    local_e = sent.shape[1]
    tiles = wide.shape[0]
    count = x_ref.shape[1]
    lanes = min(count, 128)
    if lanes < 128:
        wide[...] = jnp.zeros_like(wide)
    for j in range(tiles):
        wide[j, :x_ref.shape[0], :lanes] = x_ref[:, j * 128:j * 128 + lanes].astype(jnp.float32)
    pick = order(groups, per_dev)
    for e in range(local_e):
        rows = jnp.concatenate([wide[j, pl.ds(e, BLOCK, stride=local_e), :] for j in range(tiles)], axis=1)
        rows = rows[:, :count].astype(jnp.bfloat16)
        turned = lax.dot_general(pick, rows, NT, preferred_element_type=jnp.float32)
        flat = jnp.concatenate([turned[i * groups:(i + 1) * groups] for i in range(per_dev)], axis=1)
        for j in range(packed.shape[0]):
            packed[j, pl.ds(e, groups, stride=local_e), :] = flat[:, j * 128:(j + 1) * 128]
    for g in range(groups):
        for j in range(packed.shape[0]):
            sent[g, :, j * 128:(j + 1) * 128] = packed[j, g * local_e:(g + 1) * local_e, :].astype(jnp.bfloat16)


def unpack_kernel(groups, per_dev, landed, out_ref, wide, tall):
    local_e = landed.shape[1]
    lanes = min(out_ref.shape[1], 128)
    for g in range(groups):
        for j in range(wide.shape[0]):
            wide[j, g * local_e:(g + 1) * local_e, :] = landed[g, :, j * 128:(j + 1) * 128].astype(jnp.float32)
    pick = order(groups, per_dev)
    for e in range(local_e):
        rows = jnp.concatenate(
            [wide[j, pl.ds(e, groups, stride=local_e), :] for j in range(wide.shape[0])], axis=1)
        stack = jnp.concatenate([rows[:, i * BLOCK:(i + 1) * BLOCK] for i in range(per_dev)], axis=0)
        turned = jnp.dot(stack.T.astype(jnp.bfloat16), pick, preferred_element_type=jnp.float32)
        if lanes < 128:
            turned = jnp.concatenate([turned, jnp.zeros((BLOCK, 128 - lanes), jnp.float32)], axis=1)
        for j in range(tall.shape[0]):
            tall[j, pl.ds(e, BLOCK, stride=local_e), :] = turned[:, j * 128:(j + 1) * 128]
    for j in range(tall.shape[0]):
        out_ref[:, j * 128:j * 128 + lanes] = tall[j, :out_ref.shape[0], :lanes].astype(jnp.bfloat16)


def wire_kernel(inner, layers, side, sent, mats_in, weights_in, ints_in, back_ref,
                landed, mats, weights, ints, numbers, out_ref, green, spread_q, spread_r, both, toeplitz, bands, stage,
                slot_send, slot_recv, relay_send, relay_recv, table_send, table_recv, back_send, back_recv, local_sem):
    slots, pieces, local_e, width = landed.shape
    mine = slots - 2
    chunks = sent.shape[0]
    rows_e = pieces * local_e
    late = rows_e - WINDOW
    me, slab = lax.axis_index("energy"), lax.axis_index("slab")
    slabs = lax.axis_size("slab")
    layer, i = lax.div(me, inner), lax.rem(me, inner)
    first_of_layer = layer * inner
    first_atom = slab * (chunks * HALO) + i * (mine * HALO) - HALO
    first, last = i == 0, i == inner - 1
    below, above = layer > 0, layer < layers - 1
    slab_below, slab_above = slab > 0, slab < slabs - 1
    owner, spot = lax.div(me, layers), lax.rem(me, layers)
    barrier = pltpu.get_barrier_semaphore()
    one = lambda flag: jnp.where(flag, 1, 0)

    def hail(device, row):
        pl.semaphore_signal(barrier, inc=1, device_id=(device, row), device_id_type=MESH)

    for step in range(1, inner):
        hail(first_of_layer + partner_of(i, step), slab)

    @pl.when(first & slab_below)
    def _():
        for j in range(inner):
            hail(first_of_layer + j, slab - 1)

    @pl.when(last & slab_above)
    def _():
        for j in range(inner):
            hail(first_of_layer + j, slab + 1)

    pl.when(below)(lambda: hail(me - inner, slab))
    pl.when(above)(lambda: hail(me + inner, slab))
    for j in range(layers):
        pl.when(i * layers + j != me)(lambda: hail(i * layers + j, slab))
    pl.semaphore_wait(
        barrier, inner - 1 + one(slab_above) + one(slab_below) + one(above) + one(below) + layers - one(owner == i))

    tables = ((mats_in, mats), (weights_in, weights), (ints_in, ints))

    def table(number, j, at, to):
        src, dst = tables[number]
        return pltpu.make_async_remote_copy(
            src_ref=src, dst_ref=dst.at[at], send_sem=table_send.at[number, j], recv_sem=table_recv.at[number, at],
            device_id=(to, slab), device_id_type=MESH)

    for j in range(layers):
        to = j * inner + owner

        @pl.when(to != me)
        def _():
            for number in range(3):
                table(number, j, spot, to).start()

    def outgoing(slot, step):
        to = partner_of(i, step)
        row = slab + one((slot == 0) & (to == 0)) - one((slot == slots - 1) & (to == inner - 1))
        return pltpu.make_async_remote_copy(
            src_ref=sent.at[lax.rem(to * mine + slot - 1 + chunks, chunks)], dst_ref=landed.at[slot, side + i],
            send_sem=slot_send.at[slot, step], recv_sem=slot_recv.at[slot, step],
            device_id=(first_of_layer + to, row), device_id_type=MESH)

    def incoming(slot, step):
        source = partner_of(i, step)
        return pltpu.make_async_remote_copy(
            src_ref=sent.at[0], dst_ref=landed.at[slot, side + source],
            send_sem=slot_send.at[slot, step], recv_sem=slot_recv.at[slot, step],
            device_id=(first_of_layer + source, slab), device_id_type=MESH)

    def leaves(slot, step):
        to = partner_of(i, step)
        real = ((slot > 0) | (to > 0) | slab_above) & ((slot < slots - 1) | (to < inner - 1) | slab_below)
        if step:
            return real
        return real & (((slot == 0) & first) | ((slot == slots - 1) & last))

    def comes(slot, step):
        real = ((slot > 0) | (i > 0) | slab_below) & ((slot < slots - 1) | (i < inner - 1) | slab_above)
        if step:
            return real
        return real & (((slot == 0) & first) | ((slot == slots - 1) & last))

    def send_slot(slot, carry):
        for step in range(inner):
            pl.when(leaves(slot, step))(lambda: outgoing(slot, step).start())
        return carry

    lax.fori_loop(0, slots, send_slot, 0)

    landed[pl.ds(1, mine), side + i] = sent[pl.ds(i * mine, mine)]

    @pl.when(i > 0)
    def _():
        landed[0, side + i] = sent[lax.rem(i * mine - 1 + chunks, chunks)]

    @pl.when(i < inner - 1)
    def _():
        landed[slots - 1, side + i] = sent[lax.rem(i * mine + mine, chunks)]

    @pl.when(first & jnp.logical_not(slab_below))
    def _():
        landed[0, side:side + inner] = jnp.zeros((inner, local_e, width), landed.dtype)

    @pl.when(last & jnp.logical_not(slab_above))
    def _():
        landed[slots - 1, side:side + inner] = jnp.zeros((inner, local_e, width), landed.dtype)

    def zero(start):
        landed[:, start:start + side] = jnp.zeros((slots, side, local_e, width), landed.dtype)

    pl.when(jnp.logical_not(below))(lambda: zero(0))
    pl.when(jnp.logical_not(above))(lambda: zero(side + inner))

    @pl.when(owner == i)
    def _():
        for src, dst in tables:
            dst[spot] = src[...]

    for j in range(layers):
        @pl.when(i * layers + j != me)
        def _():
            for number in range(3):
                table(number, j, j, me).wait_recv()
    to_scalars = pltpu.make_async_copy(ints, numbers, local_sem)
    to_scalars.start()

    wide = NBR * PAIR
    lane = lax.broadcasted_iota(jnp.int32, (8, wide), 1)
    key_q = (lane // ORB)[:1]
    key_r = (lane // PAIR * ORB + lane % ORB)[:1]
    row = lax.broadcasted_iota(jnp.int32, (NBR * ORB, wide), 0)
    count = mats.shape[0] * mats.shape[1]
    matrices = mats[...].reshape(count, mats.shape[2])[:, :NBR * ORB]
    spread_q[...] = jnp.dot(matrices, (row == key_q).astype(jnp.bfloat16), preferred_element_type=jnp.float32)
    spread_r[...] = jnp.dot(matrices, (row == key_r).astype(jnp.bfloat16), preferred_element_type=jnp.float32)
    to_scalars.wait()

    def relay(way, slot):
        start, into = (inner, 0) if way == 0 else (side, side + inner)
        return pltpu.make_async_remote_copy(
            src_ref=landed.at[slot, start:start + side], dst_ref=landed.at[slot, into:into + side],
            send_sem=relay_send.at[way, slot], recv_sem=relay_recv.at[way, slot],
            device_id=(me + inner if way == 0 else me - inner, slab), device_id_type=MESH)

    def relayed(way, slot):
        into = 0 if way == 0 else side + inner
        return pltpu.make_async_remote_copy(
            src_ref=landed.at[slot, into:into + side], dst_ref=landed.at[slot, into:into + side],
            send_sem=relay_send.at[way, slot], recv_sem=relay_recv.at[way, slot],
            device_id=(me - inner if way == 0 else me + inner, slab), device_id_type=MESH)

    sub = lax.broadcasted_iota(jnp.int32, (8, WINDOW), 0)
    left_half = lax.broadcasted_iota(jnp.int32, (WINDOW, WINDOW), 1) < SPAN
    low_rows = lax.broadcasted_iota(jnp.int32, (8, wide), 0) < 4
    pair_of_atoms = 2

    def window_of(m, index):
        shift = numbers[m, 1, index]
        return shift, jnp.where(shift >= 0, 1, 0)

    def prepare(h, carry):
        m = lax.div(h, HALO // pair_of_atoms)
        for a in range(pair_of_atoms):
            atom = h * pair_of_atoms + a
            for k in range(NBR):
                index = lax.rem(atom, HALO) * NBR + k
                shift, later = window_of(m, index)
                base = shift + side * local_e - BAND // 2 - later * late
                weight = weights[m, pl.ds(index, 1), :]
                tile = pltpu.roll(jnp.broadcast_to(weight, (8, WINDOW)), WINDOW - BAND + 1 - base, 1)
                for step in (1, 2, 4):
                    tile = jnp.where((sub & step) != 0, pltpu.roll(tile, step, 1), tile)
                tiles = [tile] + [pltpu.roll(tile, 8 * b, 1) for b in range(1, WINDOW // 8)]
                band = jnp.concatenate(tiles, axis=0)
                turned_band = jnp.concatenate(tiles[SPAN // 8:] + tiles[:SPAN // 8], axis=0)
                toeplitz[atom * NBR + k, :WINDOW] = jnp.where(left_half, band, 0.0).astype(jnp.bfloat16)
                toeplitz[atom * NBR + k, WINDOW:] = jnp.where(left_half, 0.0, turned_band).astype(jnp.bfloat16)
            right = spread_r[pl.ds(pl.multiple_of(atom * 16, 16), 16), :]
            rights = (right[:8], jnp.concatenate([right[8:12], right[:4]], axis=0), right[4:12])
            for four in range(ORB // 4):
                rows = []
                for half in range(2):
                    p = four * 4 + half * 2
                    q0 = spread_q[pl.ds(atom * 16 + p, 1), :]
                    q1 = spread_q[pl.ds(atom * 16 + p + 1, 1), :]
                    rows += [q0 * rights[0], jnp.where(low_rows, q0, q1) * rights[1], q1 * rights[2]]
                both[atom, four * 48:(four + 1) * 48, :] = jnp.concatenate(rows, axis=0).astype(jnp.bfloat16)

        @pl.when(h < slots)
        def _():
            for step in range(inner):
                pl.when(comes(h, step))(lambda: incoming(h, step).wait_recv())
            pl.when(above)(lambda: relay(0, h).start())
            pl.when(below)(lambda: relay(1, h).start())
        return carry

    steps = mine * HALO // pair_of_atoms
    assert steps >= slots
    lax.fori_loop(0, steps, prepare, 0)

    unit = eye(128)

    def turn(slot, carry):
        pl.when(below)(lambda: relayed(0, slot).wait_recv())
        pl.when(above)(lambda: relayed(1, slot).wait_recv())
        if local_e % 16:
            for piece in range(pieces):
                stage[piece * local_e:(piece + 1) * local_e, :] = landed[slot, piece].astype(jnp.float32)
            tall = stage[...].astype(jnp.bfloat16)
        else:
            tall = landed[slot].reshape(rows_e, width)
        two = jnp.concatenate([tall[:WINDOW], tall[late:]], axis=0)
        turned = jnp.concatenate([
            lax.dot_general(unit, two[:, j * 128:(j + 1) * 128], NT, preferred_element_type=jnp.float32).astype(
                jnp.bfloat16) for j in range(width // 128)], axis=0)
        for atom in range(HALO):
            for c in range(2):
                start = (2 * atom + c) * PAIR
                for window in range(2):
                    green[window, slot * HALO + atom, :, c * WINDOW:(c + 1) * WINDOW] = (
                        turned[start:start + PAIR, window * WINDOW:(window + 1) * WINDOW])
        return carry

    lax.fori_loop(0, 2, turn, 0)

    def share(step, m, at):
        to = partner_of(i, step)
        return pltpu.make_async_remote_copy(
            src_ref=out_ref.at[to, m], dst_ref=back_ref.at[at * mine + m],
            send_sem=back_send.at[step, m], recv_sem=back_recv.at[step, m],
            device_id=(first_of_layer + to, slab), device_id_type=MESH)

    def chunk(m, carry):
        turn(m + 2, 0)
        for a in range(HALO):
            for k in range(NBR):
                index = a * NBR + k
                later = window_of(m, index)[1]
                partner = jnp.clip(numbers[m, 0, index] - first_atom, 0, slots * HALO - 1)
                banded = jnp.dot(
                    green[later, partner], toeplitz[m * HALO * NBR + index], preferred_element_type=jnp.float32)
                bands[a, k * PAIR:(k + 1) * PAIR, :] = banded.astype(jnp.bfloat16)
        parts = []
        for a in range(HALO):
            total = jnp.dot(both[m * HALO + a], bands[a], preferred_element_type=jnp.float32)
            turned = lax.dot_general(unit, total.astype(jnp.bfloat16), NT, preferred_element_type=jnp.float32)
            parts += [turned[:SPAN], turned[SPAN:]]
        whole = jnp.concatenate(parts, axis=1)
        for d in range(inner):
            out_ref[d, m] = whole[d * local_e:(d + 1) * local_e].astype(jnp.bfloat16)
        for step in range(1, inner):
            share(step, m, i).start()
        back_ref[i * mine + m] = out_ref[i, m]
        return carry

    lax.fori_loop(0, mine, chunk, 0)

    for j in range(layers):
        @pl.when(j * inner + owner != me)
        def _():
            for number in range(3):
                table(number, j, j, me).wait_send()

    def sent_slot(slot, carry):
        for step in range(inner):
            pl.when(leaves(slot, step))(lambda: outgoing(slot, step).wait_send())
        pl.when(above)(lambda: relay(0, slot).wait_send())
        pl.when(below)(lambda: relay(1, slot).wait_send())
        return carry

    lax.fori_loop(0, slots, sent_slot, 0)

    def finish(m, carry):
        for step in range(1, inner):
            share(step, m, partner_of(i, step)).wait_recv()
            share(step, m, i).wait_send()
        return carry

    lax.fori_loop(0, mine, finish, 0)


def on_device(green_blocks, couplings, band_weights, neighbours, shifts):
    groups = lax.axis_size("energy")
    local_e, slab_count = green_blocks.shape[3:]
    per_dev = slab_count // groups
    width = per_dev * BLOCK
    pairs = per_dev * NBR
    inner = SPAN // local_e
    layers = groups // inner
    side = pl.cdiv(REACH, local_e)
    pieces = inner + 2 * side
    mine = groups // inner
    slots = mine + 2
    assert per_dev == HALO and side <= inner and pieces * local_e >= WINDOW
    vmem = pl.BlockSpec(memory_space=pltpu.VMEM)
    smem = pl.BlockSpec(memory_space=pltpu.SMEM)
    blocks = jax.ShapeDtypeStruct((groups, local_e, width), jnp.bfloat16)
    wide = pltpu.VMEM((pl.cdiv(slab_count, 128), BLOCK * local_e, 128), jnp.float32)
    packed = pltpu.VMEM((width // 128, local_e * groups, 128), jnp.float32)
    room = pltpu.CompilerParams(vmem_limit_bytes=32 * 1024 * 1024)

    matrix = couplings.reshape(ORB, ORB, per_dev, NBR).transpose(2, 0, 3, 1).reshape(per_dev, ORB, NBR * ORB)
    matrix = jnp.pad(matrix, ((0, 0), (0, 16 - ORB), (0, 256 - NBR * ORB))).reshape(per_dev * 16, 256)
    weight = jnp.pad(band_weights.reshape(BAND, pairs)[::-1].T, ((0, 0), (0, WINDOW - BAND)))
    ints = jnp.pad(jnp.concatenate([neighbours, shifts], axis=0), ((0, 6), (0, 128 - pairs)))

    sent = pl.pallas_call(
        functools.partial(pack_kernel, groups, per_dev),
        out_shape=blocks, in_specs=[vmem], out_specs=vmem,
        scratch_shapes=[wide, packed], compiler_params=room,
    )(green_blocks.reshape(BLOCK * local_e, slab_count))

    back = pl.pallas_call(
        functools.partial(wire_kernel, inner, layers, side),
        out_shape=blocks,
        in_specs=[vmem] * 4,
        out_specs=vmem,
        scratch_shapes=[
            pltpu.VMEM((slots, pieces, local_e, width), jnp.bfloat16),
            pltpu.VMEM((layers,) + matrix.shape, jnp.bfloat16),
            pltpu.VMEM((layers,) + weight.shape, jnp.float32),
            pltpu.VMEM((layers,) + ints.shape, jnp.int32),
            pltpu.SMEM((layers,) + ints.shape, jnp.int32),
            pltpu.VMEM((inner, mine, local_e, width), jnp.bfloat16),
            pltpu.VMEM((2, slots * HALO, PAIR, 2 * WINDOW), jnp.bfloat16),
            pltpu.VMEM((mine * HALO * 16, NBR * PAIR), jnp.float32),
            pltpu.VMEM((mine * HALO * 16, NBR * PAIR), jnp.float32),
            pltpu.VMEM((mine * HALO, PAIR, NBR * PAIR), jnp.bfloat16),
            pltpu.VMEM((mine * HALO * NBR, 2 * WINDOW, WINDOW), jnp.bfloat16),
            pltpu.VMEM((HALO, NBR * PAIR, WINDOW), jnp.bfloat16),
            pltpu.VMEM((pieces * local_e, width), jnp.float32),
            pltpu.SemaphoreType.DMA((slots, inner)), pltpu.SemaphoreType.DMA((slots, inner)),
            pltpu.SemaphoreType.DMA((2, slots)), pltpu.SemaphoreType.DMA((2, slots)),
            pltpu.SemaphoreType.DMA((3, layers)), pltpu.SemaphoreType.DMA((3, layers)),
            pltpu.SemaphoreType.DMA((inner, mine)), pltpu.SemaphoreType.DMA((inner, mine)),
            pltpu.SemaphoreType.DMA,
        ],
        compiler_params=pltpu.CompilerParams(
            collective_id=0, has_side_effects=True, vmem_limit_bytes=56 * 1024 * 1024),
    )(sent, matrix, weight, ints)
    result = pl.pallas_call(
        functools.partial(unpack_kernel, groups, per_dev),
        out_shape=jax.ShapeDtypeStruct((BLOCK * local_e, slab_count), jnp.bfloat16),
        in_specs=[vmem], out_specs=vmem,
        scratch_shapes=[packed, wide], compiler_params=room,
    )(back)
    return result.reshape(2, ORB, ORB, local_e, slab_count)


def solution(mesh):
    return jax.shard_map(
        on_device,
        mesh=mesh,
        in_specs=(
            P(None, None, None, "energy", "slab"),
            P(None, None, "slab", "energy"),
            P(None, "slab", "energy"),
            P("slab", "energy"),
            P("slab", "energy"),
        ),
        out_specs=P(None, None, None, "energy", "slab"),
        check_vma=False,
    )
```

time: 77.6 us -> 78 us (level)
  the two profiles are of different devices: /device:TPU:15 before, /device:TPU:0 now
where the time goes in v3:
time: 78 us; the launch traced here: 77.7 us
  Pallas kernels  70 us (90%)
  local copies, waits for them, and re-layouts  7.02 us (9%)
    pallas_call x1, Pallas kernels, on_device(): pl.pallas_call(functools.partial(wire_kernel, inner, layers, side), out_s...  65.7 us
    unnamed x8, local copies, waits for them, and re-layouts  3.92 us
    pallas_call x1, Pallas kernels, on_device(): pl.pallas_call(functools.partial(unpack_kernel, groups, per_dev), out_sha...  2.73 us
    pallas_call x1, Pallas kernels, on_device(): pl.pallas_call(functools.partial(pack_kernel, groups, per_dev), out_shape...  1.6 us

profile of v3, /device:TPU:0, one launch (start us, length us, event | category | flops | bytes accessed | tf_op | source)
XLA Modules:
  0.0 77.7 jit_solution(13514325978845282745)
XLA Ops:
  0.0 0.7 pad_add_fusion
  0.7 0.6 pad.14.ints_in
  1.3 0.8 copy.10
  2.1 0.1 rev.3
  2.1 0.6 pad.13.weights_in
  2.7 1.0 %copy.11 = bf16[12,12,1,64]{1,3,0,2:T(8,128)(2,1)S(1)} copy(bf16[12,12,1,64]{3,1,2,0:T(8,128)(2,1)} %param.6) | data formatting | bytes 36864 | tf_op jit(solution)/shard_map/reshape | solution.py:394
  3.7 0.2 reshape.20
  3.9 0.6 pad.12.clone
  4.6 0.0 copy-start.2
  4.6 1.3 %copy-done.2 = bf16[2,12,12,16,64]{4,3,2,1,0:T(8,128)(2,1)S(1)} copy-done((bf16[2,12,12,16,64]{4,3,2,1,0:T(8,128)(2,1)S(1)}, bf16[2,12,12,16,64]{4,3,2,1,0:T(8,128)(2,1)}, u32[]{:S(2)}) %copy-start.2) | copy-done | bytes 589848
  5.8 1.6 %shard_map.55.sent = bf16[16,16,1152]{2,1,0:T(8,128)(2,1)S(1)} custom-call(bf16[4608,64]{1,0:T(8,128)(2,1)S(1)} %bitcast.12), custom_call_target="tpu_custom_call" | custom-call | tf_op jit(solution)/shard_map/pallas_call | solution.py:399
  7.4 0.0 copy-start.1
  7.5 0.8 %copy-done.1 = bf16[16,16,1152]{2,1,0:T(8,128)(2,1)} copy-done((bf16[16,16,1152]{2,1,0:T(8,128)(2,1)}, bf16[16,16,1152]{2,1,0:T(8,128)(2,1)S(1)}, u32[]{:S(2)}) %copy-start.1) | copy-done | bytes 589848
  8.3 65.7 %shard_map.56.landed = bf16[16,16,1152]{2,1,0:T(8,128)(2,1)} custom-call(bf16[16,16,1152]{2,1,0:T(8,128)(2,1)} %copy-done.1, bf16[64,256]{1,0:T(8,128)(2,1)} %bitcast.14, f32[64,128]{1,0:T(8,128)} %pad.13.weights_in, s32[8,128]{1,0:T(8,128)} %pad.14.ints_in), custom_call_target="tpu_custom_call" | custom-call | tf_op jit(solution)/shard_map/pallas_call | solution.py:405
  73.9 0.0 copy-start
  73.9 1.1 %copy-done = bf16[16,16,1152]{2,1,0:T(8,128)(2,1)S(1)} copy-done((bf16[16,16,1152]{2,1,0:T(8,128)(2,1)S(1)}, bf16[16,16,1152]{2,1,0:T(8,128)(2,1)}, u32[]{:S(2)}) %copy-start) | copy-done | bytes 589848
  75.0 2.7 %shard_map.57 = bf16[4608,64]{1,0:T(8,128)(2,1)} custom-call(bf16[16,16,1152]{2,1,0:T(8,128)(2,1)S(1)} %copy-done), custom_call_target="tpu_custom_call" | custom-call | tf_op jit(solution)/shard_map/pallas_call | solution.py:433
  (1 shorter events, 0.0 us)
Async XLA Ops:
  4.6 1.3 %copy-start.2 = (bf16[2,12,12,16,64]{4,3,2,1,0:T(8,128)(2,1)S(1)}, bf16[2,12,12,16,64]{4,3,2,1,0:T(8,128)(2,1)}, u32[]{:S(2)}) copy-start(bf16[2,12,12,16,64]{4,3,2,1,0:T(8,128)(2,1)} %param.5) | copy-start | bytes 1769476
  7.4 0.8 %copy-start.1 = (bf16[16,16,1152]{2,1,0:T(8,128)(2,1)}, bf16[16,16,1152]{2,1,0:T(8,128)(2,1)S(1)}, u32[]{:S(2)}) copy-start(bf16[16,16,1152]{2,1,0:T(8,128)(2,1)S(1)} %shard_map.55.sent) | copy-start | bytes 1769476
  73.9 1.1 %copy-start = (bf16[16,16,1152]{2,1,0:T(8,128)(2,1)S(1)}, bf16[16,16,1152]{2,1,0:T(8,128)(2,1)}, u32[]{:S(2)}) copy-start(bf16[16,16,1152]{2,1,0:T(8,128)(2,1)} %shard_map.56.landed) | copy-start | bytes 1769476

commit v4 on v3

--- a/solution.py
+++ b/solution.py
@@ -197,11 +197,11 @@
     def _():
         landed[slots - 1, side:side + inner] = jnp.zeros((inner, local_e, width), landed.dtype)
 
-    def zero(start):
+    def clear(start):
         landed[:, start:start + side] = jnp.zeros((slots, side, local_e, width), landed.dtype)
 
-    pl.when(jnp.logical_not(below))(lambda: zero(0))
-    pl.when(jnp.logical_not(above))(lambda: zero(side + inner))
+    pl.when(jnp.logical_not(below))(lambda: clear(0))
+    pl.when(jnp.logical_not(above))(lambda: clear(side + inner))
 
     @pl.when(owner == i)
     def _():
@@ -245,6 +245,7 @@
     left_half = lax.broadcasted_iota(jnp.int32, (WINDOW, WINDOW), 1) < SPAN
     low_rows = lax.broadcasted_iota(jnp.int32, (8, wide), 0) < 4
     pair_of_atoms = 2
+    zero = jnp.zeros((16, WINDOW), jnp.bfloat16)
 
     def window_of(m, index):
         shift = numbers[m, 1, index]
@@ -254,19 +255,22 @@
         m = lax.div(h, HALO // pair_of_atoms)
         for a in range(pair_of_atoms):
             atom = h * pair_of_atoms + a
+            tiles = []
             for k in range(NBR):
                 index = lax.rem(atom, HALO) * NBR + k
                 shift, later = window_of(m, index)
                 base = shift + side * local_e - BAND // 2 - later * late
                 weight = weights[m, pl.ds(index, 1), :]
-                tile = pltpu.roll(jnp.broadcast_to(weight, (8, WINDOW)), WINDOW - BAND + 1 - base, 1)
-                for step in (1, 2, 4):
-                    tile = jnp.where((sub & step) != 0, pltpu.roll(tile, step, 1), tile)
-                tiles = [tile] + [pltpu.roll(tile, 8 * b, 1) for b in range(1, WINDOW // 8)]
-                band = jnp.concatenate(tiles, axis=0)
-                turned_band = jnp.concatenate(tiles[SPAN // 8:] + tiles[:SPAN // 8], axis=0)
-                toeplitz[atom * NBR + k, :WINDOW] = jnp.where(left_half, band, 0.0).astype(jnp.bfloat16)
-                toeplitz[atom * NBR + k, WINDOW:] = jnp.where(left_half, 0.0, turned_band).astype(jnp.bfloat16)
+                tiles.append(pltpu.roll(jnp.broadcast_to(weight, (8, WINDOW)), WINDOW - BAND + 1 - base, 1))
+            for step in (1, 2, 4):
+                tiles = [jnp.where((sub & step) != 0, pltpu.roll(tile, step, 1), tile) for tile in tiles]
+            tiles = [jnp.concatenate([tile, pltpu.roll(tile, 8, 1)], axis=0).astype(jnp.bfloat16) for tile in tiles]
+            for b in range(WINDOW // 16):
+                for k in range(NBR):
+                    tile = pltpu.roll(tiles[k], 16 * b, 1) if b else tiles[k]
+                    toeplitz[atom * NBR + k, 16 * b:16 * b + 16] = jnp.where(left_half[:16], tile, zero)
+                    low = WINDOW + (16 * b - SPAN) % WINDOW
+                    toeplitz[atom * NBR + k, low:low + 16] = jnp.where(left_half[:16], zero, tile)
             right = spread_r[pl.ds(pl.multiple_of(atom * 16, 16), 16), :]
             rights = (right[:8], jnp.concatenate([right[8:12], right[:4]], axis=0), right[4:12])
             for four in range(ORB // 4):

time: 78 us -> 56 us (0.72)
  Pallas kernels: 70 us -> 48 us
    pallas_call x1, Pallas kernels: 65.7 us -> 43.6 us  [on_device(): pl.pallas_call(functools.partial(wire_kernel, inner, layers, side), out_s...]
where the time goes in v4:
time: 56 us; the launch traced here: 55.7 us
  Pallas kernels  48 us (86%)
  local copies, waits for them, and re-layouts  7.02 us (13%)
  other arithmetic  0.68 us (1%)
    pallas_call x1, Pallas kernels, on_device(): pl.pallas_call(functools.partial(wire_kernel, inner, layers, side), out_s...  43.6 us
    unnamed x8, local copies, waits for them, and re-layouts  3.92 us
    pallas_call x1, Pallas kernels, on_device(): pl.pallas_call(functools.partial(unpack_kernel, groups, per_dev), out_sha...  2.74 us
    pallas_call x1, Pallas kernels, on_device(): pl.pallas_call(functools.partial(pack_kernel, groups, per_dev), out_shape...  1.6 us
    reshape x2, local copies, waits for them, and re-layouts, on_device(): couplings.reshape(ORB, ORB, per_dev, NBR).transpose(2, 0, 3, 1)  1.18 us

profile of v4, /device:TPU:0, one launch (start us, length us, event | category | flops | bytes accessed | tf_op | source)
XLA Modules:
  0.0 55.7 jit_solution(9488160180582664013)
XLA Ops:
  0.0 0.7 %pad_add_fusion = s32[2,64]{1,0:T(2,128)S(1)} fusion(s32[1,64]{1,0:T(1,128)} %param.9, s32[1,64]{1,0:T(1,128)} %param.8), kind=kLoop, calls=%fused_computation | loop fusion | flops 128 | bytes 1024 | tf_op jit(solution)/shard_map/concatenate | solution.py:401
  0.7 0.6 %pad.14.ints_in = s32[8,128]{1,0:T(8,128)} pad(s32[2,64]{1,0:T(2,128)S(1)} %pad_add_fusion, s32[]{:T(128)} %constant.5.clone.1), padding=0_6x0_64 | pad | bytes 4612 | tf_op jit(solution)/shard_map/jit(_pad)/pad | solution.py:401
  1.3 0.8 %copy.10 = f32[9,1,64]{0,2,1:T(8,128)S(1)} copy(f32[9,1,64]{2,1,0:T(1,128)} %param.7) | data formatting | bytes 4608 | tf_op args[2]
  2.1 0.1 rev.3
  2.1 0.6 %pad.13.weights_in = f32[64,128]{1,0:T(8,128)} pad(f32[64,9]{1,0:T(8,128)S(1)} %bitcast.15, f32[]{:T(128)} %constant.4.clone.1), padding=0_0x0_119 | pad | bytes 35076 | tf_op jit(solution)/shard_map/jit(_pad)/pad | solution.py:400
  2.7 1.0 %copy.11 = bf16[12,12,1,64]{1,3,0,2:T(8,128)(2,1)S(1)} copy(bf16[12,12,1,64]{3,1,2,0:T(8,128)(2,1)} %param.6) | data formatting | bytes 36864 | tf_op jit(solution)/shard_map/reshape | solution.py:398
  3.7 0.2 reshape.20
  3.9 0.6 %pad.12.clone = bf16[4,16,256]{2,1,0:T(8,128)(2,1)} pad(bf16[4,12,192]{2,1,0:T(8,128)(2,1)S(1)} %copy.12, bf16[]{:T(256)} %constant.3.clone.1), padding=0_0x0_4x0_64 | pad | bytes 51202 | tf_op jit(solution)/shard_map/jit(_pad)/pad | solution.py:399
  4.6 0.0 copy-start.2
  4.6 1.3 %copy-done.2 = bf16[2,12,12,16,64]{4,3,2,1,0:T(8,128)(2,1)S(1)} copy-done((bf16[2,12,12,16,64]{4,3,2,1,0:T(8,128)(2,1)S(1)}, bf16[2,12,12,16,64]{4,3,2,1,0:T(8,128)(2,1)}, u32[]{:S(2)}) %copy-start.2) | copy-done | bytes 589848
  5.8 1.6 %shard_map.55.sent = bf16[16,16,1152]{2,1,0:T(8,128)(2,1)S(1)} custom-call(bf16[4608,64]{1,0:T(8,128)(2,1)S(1)} %bitcast.12), custom_call_target="tpu_custom_call" | custom-call | tf_op jit(solution)/shard_map/pallas_call | solution.py:403
  7.4 0.0 copy-start.1
  7.5 0.8 %copy-done.1 = bf16[16,16,1152]{2,1,0:T(8,128)(2,1)} copy-done((bf16[16,16,1152]{2,1,0:T(8,128)(2,1)}, bf16[16,16,1152]{2,1,0:T(8,128)(2,1)S(1)}, u32[]{:S(2)}) %copy-start.1) | copy-done | bytes 589848
  8.3 43.6 %shard_map.56.landed = bf16[16,16,1152]{2,1,0:T(8,128)(2,1)} custom-call(bf16[16,16,1152]{2,1,0:T(8,128)(2,1)} %copy-done.1, bf16[64,256]{1,0:T(8,128)(2,1)} %bitcast.14, f32[64,128]{1,0:T(8,128)} %pad.13.weights_in, s32[8,128]{1,0:T(8,128)} %pad.14.ints_in), custom_call_target="tpu_custom_call" | custom-call | tf_op jit(solution)/shard_map/pallas_call | solution.py:409
  51.9 0.0 copy-start
  51.9 1.1 %copy-done = bf16[16,16,1152]{2,1,0:T(8,128)(2,1)S(1)} copy-done((bf16[16,16,1152]{2,1,0:T(8,128)(2,1)S(1)}, bf16[16,16,1152]{2,1,0:T(8,128)(2,1)}, u32[]{:S(2)}) %copy-start) | copy-done | bytes 589848
  53.0 2.7 %shard_map.57 = bf16[4608,64]{1,0:T(8,128)(2,1)} custom-call(bf16[16,16,1152]{2,1,0:T(8,128)(2,1)S(1)} %copy-done), custom_call_target="tpu_custom_call" | custom-call | tf_op jit(solution)/shard_map/pallas_call | solution.py:437
  (1 shorter events, 0.0 us)
Async XLA Ops:
  4.6 1.3 %copy-start.2 = (bf16[2,12,12,16,64]{4,3,2,1,0:T(8,128)(2,1)S(1)}, bf16[2,12,12,16,64]{4,3,2,1,0:T(8,128)(2,1)}, u32[]{:S(2)}) copy-start(bf16[2,12,12,16,64]{4,3,2,1,0:T(8,128)(2,1)} %param.5) | copy-start | bytes 1769476
  7.4 0.8 %copy-start.1 = (bf16[16,16,1152]{2,1,0:T(8,128)(2,1)}, bf16[16,16,1152]{2,1,0:T(8,128)(2,1)S(1)}, u32[]{:S(2)}) copy-start(bf16[16,16,1152]{2,1,0:T(8,128)(2,1)S(1)} %shard_map.55.sent) | copy-start | bytes 1769476
  51.9 1.1 %copy-start = (bf16[16,16,1152]{2,1,0:T(8,128)(2,1)S(1)}, bf16[16,16,1152]{2,1,0:T(8,128)(2,1)}, u32[]{:S(2)}) copy-start(bf16[16,16,1152]{2,1,0:T(8,128)(2,1)} %shard_map.56.landed) | copy-start | bytes 1769476

commit v5 on v4

--- a/solution.py
+++ b/solution.py
@@ -85,8 +85,34 @@
         out_ref[:, j * 128:j * 128 + lanes] = tall[j, :out_ref.shape[0], :lanes].astype(jnp.bfloat16)
 
 
-def wire_kernel(inner, layers, side, sent, mats_in, weights_in, ints_in, back_ref,
-                landed, mats, weights, ints, numbers, out_ref, green, spread_q, spread_r, both, toeplitz, bands, stage,
+def table_tall(padded, weight_rows, mats_in):
+    pairs = padded.shape[2]
+    atoms, lanes = pairs // NBR, mats_in.shape[1]
+    wide = atoms * lanes
+    tall = padded[...].reshape(ORB * 16, pairs).astype(jnp.bfloat16)
+    lane = lax.broadcasted_iota(jnp.int32, (8, wide), 1)[:1]
+    inside = lane % lanes
+    pair_of = jnp.where(inside < NBR * ORB, lane // lanes * NBR + inside // ORB, -1)
+    row = lax.broadcasted_iota(jnp.int32, (pairs, wide), 0)
+    spread = jnp.dot(tall, (row == pair_of).astype(jnp.bfloat16), preferred_element_type=jnp.float32)
+    row = lax.broadcasted_iota(jnp.int32, (ORB * 16, wide), 0) % 16
+    spread = jnp.where(row == inside % ORB, spread, 0.0).astype(jnp.bfloat16)
+    p = lax.broadcasted_iota(jnp.int32, (16, ORB * 16), 0)
+    of = lax.broadcasted_iota(jnp.int32, (16, ORB * 16), 1) // 16
+    flat = jnp.dot((p == of).astype(jnp.bfloat16), spread, preferred_element_type=jnp.float32)
+    at = lax.broadcasted_iota(jnp.int32, (pairs, lanes), 1) - NBR * ORB
+    pair = lax.broadcasted_iota(jnp.int32, (pairs, lanes), 0)
+    behind = jnp.dot(
+        weight_rows[...].astype(jnp.bfloat16), (at == pair).astype(jnp.bfloat16), preferred_element_type=jnp.float32)
+    for atom in range(atoms):
+        block = flat[:, atom * lanes:(atom + 1) * lanes]
+        mats_in[atom * 16:(atom + 1) * 16, :] = (block + behind if atom == 0 else block).astype(jnp.bfloat16)
+
+
+def wire_kernel(inner, layers, side, x_ref, coupling_ref, weight_ref, near_ref, shift_ref, back_ref,
+                packed_wide, packed, sent, padded, weight_rows, mats_in,
+                landed, mats, weights, near, shifts, near_at, shift_at,
+                out_ref, green, spread_q, spread_r, both, toeplitz, bands, stage,
                 slot_send, slot_recv, relay_send, relay_recv, table_send, table_recv, back_send, back_recv, local_sem):
     slots, pieces, local_e, width = landed.shape
     mine = slots - 2
@@ -125,24 +151,53 @@
     pl.when(above)(lambda: hail(me + inner, slab))
     for j in range(layers):
         pl.when(i * layers + j != me)(lambda: hail(i * layers + j, slab))
+    pack_kernel(chunks, HALO, x_ref, sent, packed_wide, packed)
+    padded[...] = jnp.zeros_like(padded)
+    weight_rows[...] = jnp.zeros_like(weight_rows)
+    for p in range(ORB):
+        padded[p, :ORB, :] = coupling_ref[p].astype(jnp.float32)
+    weight_rows[:BAND, :] = weight_ref[:, 0, :]
+    table_tall(padded, weight_rows, mats_in)
+
+    landed[pl.ds(1, mine), side + i] = sent[pl.ds(i * mine, mine)]
+
+    @pl.when(i > 0)
+    def _():
+        landed[0, side + i] = sent[lax.rem(i * mine - 1 + chunks, chunks)]
+
+    @pl.when(i < inner - 1)
+    def _():
+        landed[slots - 1, side + i] = sent[lax.rem(i * mine + mine, chunks)]
+
+    @pl.when(first & jnp.logical_not(slab_below))
+    def _():
+        landed[0, side:side + inner] = jnp.zeros((inner, local_e, width), landed.dtype)
+
+    @pl.when(last & jnp.logical_not(slab_above))
+    def _():
+        landed[slots - 1, side:side + inner] = jnp.zeros((inner, local_e, width), landed.dtype)
+
+    def clear(start):
+        landed[:, start:start + side] = jnp.zeros((slots, side, local_e, width), landed.dtype)
+
+    pl.when(jnp.logical_not(below))(lambda: clear(0))
+    pl.when(jnp.logical_not(above))(lambda: clear(side + inner))
+
+    tables = ((mats_in, mats), (near_ref, near), (shift_ref, shifts))
+
+    @pl.when(owner == i)
+    def _():
+        for src, dst in tables:
+            dst[spot] = src[...]
+
     pl.semaphore_wait(
         barrier, inner - 1 + one(slab_above) + one(slab_below) + one(above) + one(below) + layers - one(owner == i))
-
-    tables = ((mats_in, mats), (weights_in, weights), (ints_in, ints))
 
     def table(number, j, at, to):
         src, dst = tables[number]
         return pltpu.make_async_remote_copy(
             src_ref=src, dst_ref=dst.at[at], send_sem=table_send.at[number, j], recv_sem=table_recv.at[number, at],
             device_id=(to, slab), device_id_type=MESH)
-
-    for j in range(layers):
-        to = j * inner + owner
-
-        @pl.when(to != me)
-        def _():
-            for number in range(3):
-                table(number, j, spot, to).start()
 
     def outgoing(slot, step):
         to = partner_of(i, step)
@@ -177,44 +232,55 @@
             pl.when(leaves(slot, step))(lambda: outgoing(slot, step).start())
         return carry
 
-    lax.fori_loop(0, slots, send_slot, 0)
-
-    landed[pl.ds(1, mine), side + i] = sent[pl.ds(i * mine, mine)]
-
-    @pl.when(i > 0)
-    def _():
-        landed[0, side + i] = sent[lax.rem(i * mine - 1 + chunks, chunks)]
-
-    @pl.when(i < inner - 1)
-    def _():
-        landed[slots - 1, side + i] = sent[lax.rem(i * mine + mine, chunks)]
-
-    @pl.when(first & jnp.logical_not(slab_below))
-    def _():
-        landed[0, side:side + inner] = jnp.zeros((inner, local_e, width), landed.dtype)
-
-    @pl.when(last & jnp.logical_not(slab_above))
-    def _():
-        landed[slots - 1, side:side + inner] = jnp.zeros((inner, local_e, width), landed.dtype)
-
-    def clear(start):
-        landed[:, start:start + side] = jnp.zeros((slots, side, local_e, width), landed.dtype)
-
-    pl.when(jnp.logical_not(below))(lambda: clear(0))
-    pl.when(jnp.logical_not(above))(lambda: clear(side + inner))
-
-    @pl.when(owner == i)
-    def _():
-        for src, dst in tables:
-            dst[spot] = src[...]
-
+    lax.fori_loop(0, 3, send_slot, 0)
+    for j in range(layers):
+        to = j * inner + owner
+
+        @pl.when(to != me)
+        def _():
+            for number in range(3):
+                table(number, j, spot, to).start()
+
+    lax.fori_loop(3, slots, send_slot, 0)
+
+    def relay(way, slot):
+        start, into = (inner, 0) if way == 0 else (side, side + inner)
+        return pltpu.make_async_remote_copy(
+            src_ref=landed.at[slot, start:start + side], dst_ref=landed.at[slot, into:into + side],
+            send_sem=relay_send.at[way, slot], recv_sem=relay_recv.at[way, slot],
+            device_id=(me + inner if way == 0 else me - inner, slab), device_id_type=MESH)
+
+    def relayed(way, slot):
+        into = 0 if way == 0 else side + inner
+        return pltpu.make_async_remote_copy(
+            src_ref=landed.at[slot, into:into + side], dst_ref=landed.at[slot, into:into + side],
+            send_sem=relay_send.at[way, slot], recv_sem=relay_recv.at[way, slot],
+            device_id=(me - inner if way == 0 else me + inner, slab), device_id_type=MESH)
+
+    def pass_on(slot):
+        for step in range(inner):
+            pl.when(comes(slot, step))(lambda: incoming(slot, step).wait_recv())
+        pl.when(above)(lambda: relay(0, slot).start())
+        pl.when(below)(lambda: relay(1, slot).start())
+
+    pass_on(0)
     for j in range(layers):
         @pl.when(i * layers + j != me)
         def _():
             for number in range(3):
                 table(number, j, j, me).wait_recv()
-    to_scalars = pltpu.make_async_copy(ints, numbers, local_sem)
-    to_scalars.start()
+    to_scalars = (pltpu.make_async_copy(near, near_at, local_sem.at[0]),
+                  pltpu.make_async_copy(shifts, shift_at, local_sem.at[1]))
+    for copy in to_scalars:
+        copy.start()
+    lane_of = lax.broadcasted_iota(jnp.int32, (16, WINDOW), 1)
+    row_of = lax.broadcasted_iota(jnp.int32, (16, WINDOW), 0)
+    place = ((lane_of + row_of == BAND - 1) & (row_of < BAND)).astype(jnp.bfloat16)
+    count_pairs = mats.shape[2] - NBR * ORB
+    for j in range(layers):
+        column = lax.dot_general(
+            eye(count_pairs), mats[j, :16, NBR * ORB:], NT, preferred_element_type=jnp.float32).astype(jnp.bfloat16)
+        weights[j] = jnp.dot(column, place, preferred_element_type=jnp.float32)
 
     wide = NBR * PAIR
     lane = lax.broadcasted_iota(jnp.int32, (8, wide), 1)
@@ -224,22 +290,11 @@
     count = mats.shape[0] * mats.shape[1]
     matrices = mats[...].reshape(count, mats.shape[2])[:, :NBR * ORB]
     spread_q[...] = jnp.dot(matrices, (row == key_q).astype(jnp.bfloat16), preferred_element_type=jnp.float32)
+    pass_on(1)
     spread_r[...] = jnp.dot(matrices, (row == key_r).astype(jnp.bfloat16), preferred_element_type=jnp.float32)
-    to_scalars.wait()
-
-    def relay(way, slot):
-        start, into = (inner, 0) if way == 0 else (side, side + inner)
-        return pltpu.make_async_remote_copy(
-            src_ref=landed.at[slot, start:start + side], dst_ref=landed.at[slot, into:into + side],
-            send_sem=relay_send.at[way, slot], recv_sem=relay_recv.at[way, slot],
-            device_id=(me + inner if way == 0 else me - inner, slab), device_id_type=MESH)
-
-    def relayed(way, slot):
-        into = 0 if way == 0 else side + inner
-        return pltpu.make_async_remote_copy(
-            src_ref=landed.at[slot, into:into + side], dst_ref=landed.at[slot, into:into + side],
-            send_sem=relay_send.at[way, slot], recv_sem=relay_recv.at[way, slot],
-            device_id=(me - inner if way == 0 else me + inner, slab), device_id_type=MESH)
+    for copy in to_scalars:
+        copy.wait()
+    pass_on(2)
 
     sub = lax.broadcasted_iota(jnp.int32, (8, WINDOW), 0)
     left_half = lax.broadcasted_iota(jnp.int32, (WINDOW, WINDOW), 1) < SPAN
@@ -248,7 +303,7 @@
     zero = jnp.zeros((16, WINDOW), jnp.bfloat16)
 
     def window_of(m, index):
-        shift = numbers[m, 1, index]
+        shift = shift_at[m, 0, index]
         return shift, jnp.where(shift >= 0, 1, 0)
 
     def prepare(h, carry):
@@ -282,12 +337,7 @@
                     rows += [q0 * rights[0], jnp.where(low_rows, q0, q1) * rights[1], q1 * rights[2]]
                 both[atom, four * 48:(four + 1) * 48, :] = jnp.concatenate(rows, axis=0).astype(jnp.bfloat16)
 
-        @pl.when(h < slots)
-        def _():
-            for step in range(inner):
-                pl.when(comes(h, step))(lambda: incoming(h, step).wait_recv())
-            pl.when(above)(lambda: relay(0, h).start())
-            pl.when(below)(lambda: relay(1, h).start())
+        pl.when(h < slots - 3)(lambda: pass_on(h + 3))
         return carry
 
     steps = mine * HALO // pair_of_atoms
@@ -332,7 +382,7 @@
             for k in range(NBR):
                 index = a * NBR + k
                 later = window_of(m, index)[1]
-                partner = jnp.clip(numbers[m, 0, index] - first_atom, 0, slots * HALO - 1)
+                partner = jnp.clip(near_at[m, 0, index] - first_atom, 0, slots * HALO - 1)
                 banded = jnp.dot(
                     green[later, partner], toeplitz[m * HALO * NBR + index], preferred_element_type=jnp.float32)
                 bands[a, k * PAIR:(k + 1) * PAIR, :] = banded.astype(jnp.bfloat16)
@@ -381,6 +431,7 @@
     per_dev = slab_count // groups
     width = per_dev * BLOCK
     pairs = per_dev * NBR
+    lanes = NBR * ORB + pairs
     inner = SPAN // local_e
     layers = groups // inner
     side = pl.cdiv(REACH, local_e)
@@ -395,28 +446,22 @@
     packed = pltpu.VMEM((width // 128, local_e * groups, 128), jnp.float32)
     room = pltpu.CompilerParams(vmem_limit_bytes=32 * 1024 * 1024)
 
-    matrix = couplings.reshape(ORB, ORB, per_dev, NBR).transpose(2, 0, 3, 1).reshape(per_dev, ORB, NBR * ORB)
-    matrix = jnp.pad(matrix, ((0, 0), (0, 16 - ORB), (0, 256 - NBR * ORB))).reshape(per_dev * 16, 256)
-    weight = jnp.pad(band_weights.reshape(BAND, pairs)[::-1].T, ((0, 0), (0, WINDOW - BAND)))
-    ints = jnp.pad(jnp.concatenate([neighbours, shifts], axis=0), ((0, 6), (0, 128 - pairs)))
-
-    sent = pl.pallas_call(
-        functools.partial(pack_kernel, groups, per_dev),
-        out_shape=blocks, in_specs=[vmem], out_specs=vmem,
-        scratch_shapes=[wide, packed], compiler_params=room,
-    )(green_blocks.reshape(BLOCK * local_e, slab_count))
-
     back = pl.pallas_call(
         functools.partial(wire_kernel, inner, layers, side),
         out_shape=blocks,
-        in_specs=[vmem] * 4,
+        in_specs=[vmem] * 5,
         out_specs=vmem,
         scratch_shapes=[
+            wide, packed, pltpu.VMEM(blocks.shape, jnp.bfloat16),
+            pltpu.VMEM((ORB, 16, pairs), jnp.float32), pltpu.VMEM((16, pairs), jnp.float32),
+            pltpu.VMEM((per_dev * 16, lanes), jnp.bfloat16),
             pltpu.VMEM((slots, pieces, local_e, width), jnp.bfloat16),
-            pltpu.VMEM((layers,) + matrix.shape, jnp.bfloat16),
-            pltpu.VMEM((layers,) + weight.shape, jnp.float32),
-            pltpu.VMEM((layers,) + ints.shape, jnp.int32),
-            pltpu.SMEM((layers,) + ints.shape, jnp.int32),
+            pltpu.VMEM((layers, per_dev * 16, lanes), jnp.bfloat16),
+            pltpu.VMEM((layers, pairs, WINDOW), jnp.float32),
+            pltpu.VMEM((layers, 1, pairs), jnp.int32),
+            pltpu.VMEM((layers, 1, pairs), jnp.int32),
+            pltpu.SMEM((layers, 1, pairs), jnp.int32),
+            pltpu.SMEM((layers, 1, pairs), jnp.int32),
             pltpu.VMEM((inner, mine, local_e, width), jnp.bfloat16),
             pltpu.VMEM((2, slots * HALO, PAIR, 2 * WINDOW), jnp.bfloat16),
             pltpu.VMEM((mine * HALO * 16, NBR * PAIR), jnp.float32),
@@ -424,16 +469,16 @@
             pltpu.VMEM((mine * HALO, PAIR, NBR * PAIR), jnp.bfloat16),
             pltpu.VMEM((mine * HALO * NBR, 2 * WINDOW, WINDOW), jnp.bfloat16),
             pltpu.VMEM((HALO, NBR * PAIR, WINDOW), jnp.bfloat16),
-            pltpu.VMEM((pieces * local_e, width), jnp.float32),
+            pltpu.VMEM((pieces * local_e if local_e % 16 else 8, width), jnp.float32),
             pltpu.SemaphoreType.DMA((slots, inner)), pltpu.SemaphoreType.DMA((slots, inner)),
             pltpu.SemaphoreType.DMA((2, slots)), pltpu.SemaphoreType.DMA((2, slots)),
             pltpu.SemaphoreType.DMA((3, layers)), pltpu.SemaphoreType.DMA((3, layers)),
             pltpu.SemaphoreType.DMA((inner, mine)), pltpu.SemaphoreType.DMA((inner, mine)),
-            pltpu.SemaphoreType.DMA,
+            pltpu.SemaphoreType.DMA((2,)),
         ],
         compiler_params=pltpu.CompilerParams(
-            collective_id=0, has_side_effects=True, vmem_limit_bytes=56 * 1024 * 1024),
-    )(sent, matrix, weight, ints)
+            collective_id=0, has_side_effects=True, vmem_limit_bytes=48 * 1024 * 1024),
+    )(green_blocks.reshape(BLOCK * local_e, slab_count), couplings.reshape(ORB, ORB, pairs), band_weights, neighbours, shifts)
     result = pl.pallas_call(
         functools.partial(unpack_kernel, groups, per_dev),
         out_shape=jax.ShapeDtypeStruct((BLOCK * local_e, slab_count), jnp.bfloat16),

time: 56 us -> 48.4 us (0.86)
  Pallas kernels: 48 us -> 44.1 us
  local copies, waits for them, and re-layouts: 7.02 us -> 4.06 us
  other arithmetic: 0.68 us -> 0 us
    pallas_call x1, Pallas kernels: 43.6 us -> 41.3 us  [on_device(): pl.pallas_call(functools.partial(wire_kernel, inner, layers, side), out_s...]
    pad x3 -> x0, local copies, waits for them, and re-layouts: 1.84 us -> none  [the longest x1 0.62 us: on_device(): jnp.pad(matrix, ((0, 0), (0, 16 - ORB), (0, 256 - NBR * ORB)))]
    pallas_call x1 -> x0, Pallas kernels: 1.6 us -> none  [on_device(): pl.pallas_call(functools.partial(pack_kernel, groups, per_dev), out_shape...]
    reshape x2 -> x0, local copies, waits for them, and re-layouts: 1.18 us -> none  [on_device(): couplings.reshape(ORB, ORB, per_dev, NBR).transpose(2, 0, 3, 1)]
    concatenate x1 -> x0, other arithmetic: 0.68 us -> none  [on_device(): jnp.concatenate([neighbours, shifts], axis=0)]
    unnamed x8 -> x10, local copies, waits for them, and re-layouts: 3.92 us -> 4.06 us
where the time goes in v5:
time: 48.4 us; the launch traced here: 48.1 us
  Pallas kernels  44.1 us (91%)
  local copies, waits for them, and re-layouts  4.06 us (8%)
    pallas_call x1, Pallas kernels, on_device(): pl.pallas_call(functools.partial(wire_kernel, inner, layers, side), out_s...  41.3 us
    unnamed x10, local copies, waits for them, and re-layouts  4.06 us
    pallas_call x1, Pallas kernels, on_device(): pl.pallas_call(functools.partial(unpack_kernel, groups, per_dev), out_sha...  2.74 us

profile of v5, /device:TPU:0, one launch (start us, length us, event | category | flops | bytes accessed | tf_op | source)
XLA Modules:
  0.0 48.1 jit_solution(13500443937102229821)
XLA Ops:
  0.0 0.0 copy-start
  0.0 1.3 %copy-done = bf16[2,12,12,16,64]{4,3,2,1,0:T(8,128)(2,1)S(1)} copy-done((bf16[2,12,12,16,64]{4,3,2,1,0:T(8,128)(2,1)S(1)}, bf16[2,12,12,16,64]{4,3,2,1,0:T(8,128)(2,1)}, u32[]{:S(2)}) %copy-start) | copy-done | bytes 589848
  1.3 0.0 copy-start.1
  1.3 0.8 %copy-done.1 = bf16[12,12,1,64]{3,1,2,0:T(8,128)(2,1)S(1)} copy-done((bf16[12,12,1,64]{3,1,2,0:T(8,128)(2,1)S(1)}, bf16[12,12,1,64]{3,1,2,0:T(8,128)(2,1)}, u32[]{:S(2)}) %copy-start.1) | copy-done | bytes 18456
  2.1 0.0 copy-start.2
  2.1 0.7 %copy-done.2 = f32[9,1,64]{2,1,0:T(1,128)S(1)} copy-done((f32[9,1,64]{2,1,0:T(1,128)S(1)}, f32[9,1,64]{2,1,0:T(1,128)}, u32[]{:S(2)}) %copy-start.2) | copy-done | bytes 2328
  2.8 0.0 copy-start.3
  2.8 0.7 %copy-done.3 = s32[1,64]{1,0:T(1,128)S(1)} copy-done((s32[1,64]{1,0:T(1,128)S(1)}, s32[1,64]{1,0:T(1,128)}, u32[]{:S(2)}) %copy-start.3) | copy-done | bytes 280
  3.4 0.0 copy-start.4
  3.4 0.7 %copy-done.4 = s32[1,64]{1,0:T(1,128)S(1)} copy-done((s32[1,64]{1,0:T(1,128)S(1)}, s32[1,64]{1,0:T(1,128)}, u32[]{:S(2)}) %copy-start.4) | copy-done | bytes 280
  4.1 41.3 %shard_map.55.landed = bf16[16,16,1152]{2,1,0:T(8,128)(2,1)S(1)} custom-call(bf16[4608,64]{1,0:T(8,128)(2,1)S(1)} %bitcast.3, bf16[12,12,64]{2,1,0:T(8,128)(2,1)S(1)} %bitcast.4, f32[9,1,64]{2,1,0:T(1,128)S(1)} %copy-done.2, s32[1,64]{1,0:T(1,128)S(1)} %copy-done.3, s32[1,64]{1,0:T(1,128)S(1)} %copy-done.4), custom_call_target="tpu_custom_call" | custom-call | tf_op jit(solution)/shard_map/pallas_call | solution.py:449
  45.4 2.7 %shard_map.56 = bf16[4608,64]{1,0:T(8,128)(2,1)} custom-call(bf16[16,16,1152]{2,1,0:T(8,128)(2,1)S(1)} %shard_map.55.landed), custom_call_target="tpu_custom_call" | custom-call | tf_op jit(solution)/shard_map/pallas_call | solution.py:482
Async XLA Ops:
  0.0 1.3 %copy-start = (bf16[2,12,12,16,64]{4,3,2,1,0:T(8,128)(2,1)S(1)}, bf16[2,12,12,16,64]{4,3,2,1,0:T(8,128)(2,1)}, u32[]{:S(2)}) copy-start(bf16[2,12,12,16,64]{4,3,2,1,0:T(8,128)(2,1)} %param.5) | copy-start | bytes 1769476
  1.3 0.8 %copy-start.1 = (bf16[12,12,1,64]{3,1,2,0:T(8,128)(2,1)S(1)}, bf16[12,12,1,64]{3,1,2,0:T(8,128)(2,1)}, u32[]{:S(2)}) copy-start(bf16[12,12,1,64]{3,1,2,0:T(8,128)(2,1)} %param.6) | copy-start | bytes 55300
  2.1 0.7 %copy-start.2 = (f32[9,1,64]{2,1,0:T(1,128)S(1)}, f32[9,1,64]{2,1,0:T(1,128)}, u32[]{:S(2)}) copy-start(f32[9,1,64]{2,1,0:T(1,128)} %weight_ref.1) | copy-start | bytes 6916
  2.8 0.7 %copy-start.3 = (s32[1,64]{1,0:T(1,128)S(1)}, s32[1,64]{1,0:T(1,128)}, u32[]{:S(2)}) copy-start(s32[1,64]{1,0:T(1,128)} %near_ref.1) | copy-start | bytes 772
  3.4 0.7 %copy-start.4 = (s32[1,64]{1,0:T(1,128)S(1)}, s32[1,64]{1,0:T(1,128)}, u32[]{:S(2)}) copy-start(s32[1,64]{1,0:T(1,128)} %shift_ref.1) | copy-start | bytes 772

commit v6 on v5

--- a/solution.py
+++ b/solution.py
@@ -109,9 +109,9 @@
         mats_in[atom * 16:(atom + 1) * 16, :] = (block + behind if atom == 0 else block).astype(jnp.bfloat16)
 
 
-def wire_kernel(inner, layers, side, x_ref, coupling_ref, weight_ref, near_ref, shift_ref, back_ref,
-                packed_wide, packed, sent, padded, weight_rows, mats_in,
-                landed, mats, weights, near, shifts, near_at, shift_at,
+def wire_kernel(inner, layers, side, sent, coupling_ref, weight_ref, near_ref, shift_ref, back_ref,
+                padded, weight_rows, mats_in,
+                landed, mats, weights, near, shifts, near_at, shift_at, pick_q, pick_r,
                 out_ref, green, spread_q, spread_r, both, toeplitz, bands, stage,
                 slot_send, slot_recv, relay_send, relay_recv, table_send, table_recv, back_send, back_recv, local_sem):
     slots, pieces, local_e, width = landed.shape
@@ -151,7 +151,6 @@
     pl.when(above)(lambda: hail(me + inner, slab))
     for j in range(layers):
         pl.when(i * layers + j != me)(lambda: hail(i * layers + j, slab))
-    pack_kernel(chunks, HALO, x_ref, sent, packed_wide, packed)
     padded[...] = jnp.zeros_like(padded)
     weight_rows[...] = jnp.zeros_like(weight_rows)
     for p in range(ORB):
@@ -241,7 +240,13 @@
             for number in range(3):
                 table(number, j, spot, to).start()
 
-    lax.fori_loop(3, slots, send_slot, 0)
+    wide = NBR * PAIR
+    lane = lax.broadcasted_iota(jnp.int32, (8, wide), 1)
+    key_q = (lane // ORB)[:1]
+    key_r = (lane // PAIR * ORB + lane % ORB)[:1]
+    row = lax.broadcasted_iota(jnp.int32, (NBR * ORB, wide), 0)
+    pick_q[...] = (row == key_q).astype(jnp.bfloat16)
+    pick_r[...] = (row == key_r).astype(jnp.bfloat16)
 
     def relay(way, slot):
         start, into = (inner, 0) if way == 0 else (side, side + inner)
@@ -264,6 +269,7 @@
         pl.when(below)(lambda: relay(1, slot).start())
 
     pass_on(0)
+    send_slot(3, 0)
     for j in range(layers):
         @pl.when(i * layers + j != me)
         def _():
@@ -282,19 +288,16 @@
             eye(count_pairs), mats[j, :16, NBR * ORB:], NT, preferred_element_type=jnp.float32).astype(jnp.bfloat16)
         weights[j] = jnp.dot(column, place, preferred_element_type=jnp.float32)
 
-    wide = NBR * PAIR
-    lane = lax.broadcasted_iota(jnp.int32, (8, wide), 1)
-    key_q = (lane // ORB)[:1]
-    key_r = (lane // PAIR * ORB + lane % ORB)[:1]
-    row = lax.broadcasted_iota(jnp.int32, (NBR * ORB, wide), 0)
     count = mats.shape[0] * mats.shape[1]
     matrices = mats[...].reshape(count, mats.shape[2])[:, :NBR * ORB]
-    spread_q[...] = jnp.dot(matrices, (row == key_q).astype(jnp.bfloat16), preferred_element_type=jnp.float32)
+    spread_q[...] = jnp.dot(matrices, pick_q[...], preferred_element_type=jnp.float32)
     pass_on(1)
-    spread_r[...] = jnp.dot(matrices, (row == key_r).astype(jnp.bfloat16), preferred_element_type=jnp.float32)
+    send_slot(4, 0)
+    spread_r[...] = jnp.dot(matrices, pick_r[...], preferred_element_type=jnp.float32)
     for copy in to_scalars:
         copy.wait()
     pass_on(2)
+    send_slot(5, 0)
 
     sub = lax.broadcasted_iota(jnp.int32, (8, WINDOW), 0)
     left_half = lax.broadcasted_iota(jnp.int32, (WINDOW, WINDOW), 1) < SPAN
@@ -337,11 +340,11 @@
                     rows += [q0 * rights[0], jnp.where(low_rows, q0, q1) * rights[1], q1 * rights[2]]
                 both[atom, four * 48:(four + 1) * 48, :] = jnp.concatenate(rows, axis=0).astype(jnp.bfloat16)
 
-        pl.when(h < slots - 3)(lambda: pass_on(h + 3))
+        pl.when((h % 2 == 1) & (h < 6))(lambda: pass_on(lax.div(h, 2) + 3))
         return carry
 
     steps = mine * HALO // pair_of_atoms
-    assert steps >= slots
+    assert slots == 6 and steps >= slots
     lax.fori_loop(0, steps, prepare, 0)
 
     unit = eye(128)
@@ -446,13 +449,17 @@
     packed = pltpu.VMEM((width // 128, local_e * groups, 128), jnp.float32)
     room = pltpu.CompilerParams(vmem_limit_bytes=32 * 1024 * 1024)
 
+    sent = pl.pallas_call(
+        functools.partial(pack_kernel, groups, per_dev),
+        out_shape=blocks, in_specs=[vmem], out_specs=vmem,
+        scratch_shapes=[wide, packed], compiler_params=room,
+    )(green_blocks.reshape(BLOCK * local_e, slab_count))
     back = pl.pallas_call(
         functools.partial(wire_kernel, inner, layers, side),
         out_shape=blocks,
         in_specs=[vmem] * 5,
         out_specs=vmem,
         scratch_shapes=[
-            wide, packed, pltpu.VMEM(blocks.shape, jnp.bfloat16),
             pltpu.VMEM((ORB, 16, pairs), jnp.float32), pltpu.VMEM((16, pairs), jnp.float32),
             pltpu.VMEM((per_dev * 16, lanes), jnp.bfloat16),
             pltpu.VMEM((slots, pieces, local_e, width), jnp.bfloat16),
@@ -462,6 +469,7 @@
             pltpu.VMEM((layers, 1, pairs), jnp.int32),
             pltpu.SMEM((layers, 1, pairs), jnp.int32),
             pltpu.SMEM((layers, 1, pairs), jnp.int32),
+            pltpu.VMEM((NBR * ORB, NBR * PAIR), jnp.bfloat16), pltpu.VMEM((NBR * ORB, NBR * PAIR), jnp.bfloat16),
             pltpu.VMEM((inner, mine, local_e, width), jnp.bfloat16),
             pltpu.VMEM((2, slots * HALO, PAIR, 2 * WINDOW), jnp.bfloat16),
             pltpu.VMEM((mine * HALO * 16, NBR * PAIR), jnp.float32),
@@ -478,7 +486,7 @@
         ],
         compiler_params=pltpu.CompilerParams(
             collective_id=0, has_side_effects=True, vmem_limit_bytes=48 * 1024 * 1024),
-    )(green_blocks.reshape(BLOCK * local_e, slab_count), couplings.reshape(ORB, ORB, pairs), band_weights, neighbours, shifts)
+    )(sent, couplings.reshape(ORB, ORB, pairs), band_weights, neighbours, shifts)
     result = pl.pallas_call(
         functools.partial(unpack_kernel, groups, per_dev),
         out_shape=jax.ShapeDtypeStruct((BLOCK * local_e, slab_count), jnp.bfloat16),

time: 48.4 us -> 46.3 us (0.957)
  local copies, waits for them, and re-layouts: 4.06 us -> 1.31 us
  Pallas kernels: 44.1 us -> 44.8 us
    unnamed x10, local copies, waits for them, and re-layouts: 4.06 us -> 1.31 us
    pallas_call x0 -> x1, Pallas kernels: none -> 1.6 us  [on_device(): pl.pallas_call(functools.partial(pack_kernel, groups, per_dev), out_shape...]
    pallas_call x1, Pallas kernels: 41.3 us -> 40.5 us  [on_device(): pl.pallas_call(functools.partial(wire_kernel, inner, layers, side), out_s...]
where the time goes in v6:
time: 46.3 us; the launch traced here: 46.2 us
  Pallas kernels  44.8 us (97%)
  local copies, waits for them, and re-layouts  1.31 us (3%)
    pallas_call x1, Pallas kernels, on_device(): pl.pallas_call(functools.partial(wire_kernel, inner, layers, side), out_s...  40.5 us
    pallas_call x1, Pallas kernels, on_device(): pl.pallas_call(functools.partial(unpack_kernel, groups, per_dev), out_sha...  2.74 us
    pallas_call x1, Pallas kernels, on_device(): pl.pallas_call(functools.partial(pack_kernel, groups, per_dev), out_shape...  1.6 us
    unnamed x10, local copies, waits for them, and re-layouts  1.31 us

profile of v6, /device:TPU:0, one launch (start us, length us, event | category | flops | bytes accessed | tf_op | source)
XLA Modules:
  0.0 46.2 jit_solution(18054912344370990572)
XLA Ops:
  0.0 0.0 copy-start.4
  0.0 0.0 copy-start.3
  0.0 0.0 copy-start
  0.0 1.3 %copy-done = bf16[2,12,12,16,64]{4,3,2,1,0:T(8,128)(2,1)S(1)} copy-done((bf16[2,12,12,16,64]{4,3,2,1,0:T(8,128)(2,1)S(1)}, bf16[2,12,12,16,64]{4,3,2,1,0:T(8,128)(2,1)}, u32[]{:S(2)}) %copy-start) | copy-done | bytes 589848
  1.3 0.0 copy-start.1
  1.3 0.0 copy-start.2
  1.3 1.6 %shard_map.55.sent = bf16[16,16,1152]{2,1,0:T(8,128)(2,1)S(1)} custom-call(bf16[4608,64]{1,0:T(8,128)(2,1)S(1)} %bitcast.3), custom_call_target="tpu_custom_call" | custom-call | tf_op jit(solution)/shard_map/pallas_call | solution.py:452
  2.9 0.0 copy-done.4
  2.9 0.0 copy-done.3
  2.9 0.0 copy-done.1
  2.9 0.0 copy-done.2
  3.0 40.5 %shard_map.56.landed = bf16[16,16,1152]{2,1,0:T(8,128)(2,1)S(1)} custom-call(bf16[16,16,1152]{2,1,0:T(8,128)(2,1)S(1)} %shard_map.55.sent, bf16[12,12,64]{2,1,0:T(8,128)(2,1)S(1)} %bitcast.4, f32[9,1,64]{2,1,0:T(1,128)S(1)} %copy-done.2, s32[1,64]{1,0:T(1,128)S(1)} %copy-done.3, s32[1,64]{1,0:T(1,128)S(1)} %copy-done.4), custom_call_target="tpu_custom_call" | custom-call | tf_op jit(solution)/shard_map/pallas_call | solution.py:457
  43.4 2.7 %shard_map.57 = bf16[4608,64]{1,0:T(8,128)(2,1)} custom-call(bf16[16,16,1152]{2,1,0:T(8,128)(2,1)S(1)} %shard_map.56.landed), custom_call_target="tpu_custom_call" | custom-call | tf_op jit(solution)/shard_map/pallas_call | solution.py:490
Async XLA Ops:
  0.0 2.9 %copy-start.4 = (s32[1,64]{1,0:T(1,128)S(1)}, s32[1,64]{1,0:T(1,128)}, u32[]{:S(2)}) copy-start(s32[1,64]{1,0:T(1,128)} %shift_ref.1) | copy-start | bytes 772
  0.0 2.9 %copy-start.3 = (s32[1,64]{1,0:T(1,128)S(1)}, s32[1,64]{1,0:T(1,128)}, u32[]{:S(2)}) copy-start(s32[1,64]{1,0:T(1,128)} %near_ref.1) | copy-start | bytes 772
  0.0 1.3 %copy-start = (bf16[2,12,12,16,64]{4,3,2,1,0:T(8,128)(2,1)S(1)}, bf16[2,12,12,16,64]{4,3,2,1,0:T(8,128)(2,1)}, u32[]{:S(2)}) copy-start(bf16[2,12,12,16,64]{4,3,2,1,0:T(8,128)(2,1)} %param.5) | copy-start | bytes 1769476
  1.3 1.6 %copy-start.1 = (bf16[12,12,1,64]{3,1,2,0:T(8,128)(2,1)S(1)}, bf16[12,12,1,64]{3,1,2,0:T(8,128)(2,1)}, u32[]{:S(2)}) copy-start(bf16[12,12,1,64]{3,1,2,0:T(8,128)(2,1)} %param.6) | copy-start | bytes 55300
  1.3 1.6 %copy-start.2 = (f32[9,1,64]{2,1,0:T(1,128)S(1)}, f32[9,1,64]{2,1,0:T(1,128)}, u32[]{:S(2)}) copy-start(f32[9,1,64]{2,1,0:T(1,128)} %weight_ref.1) | copy-start | bytes 6916

commit v7 on v6

--- a/solution.py
+++ b/solution.py
@@ -231,7 +231,6 @@
             pl.when(leaves(slot, step))(lambda: outgoing(slot, step).start())
         return carry
 
-    lax.fori_loop(0, 3, send_slot, 0)
     for j in range(layers):
         to = j * inner + owner
 
@@ -239,6 +238,8 @@
         def _():
             for number in range(3):
                 table(number, j, spot, to).start()
+
+    lax.fori_loop(0, 3, send_slot, 0)
 
     wide = NBR * PAIR
     lane = lax.broadcasted_iota(jnp.int32, (8, wide), 1)
@@ -268,8 +269,6 @@
         pl.when(above)(lambda: relay(0, slot).start())
         pl.when(below)(lambda: relay(1, slot).start())
 
-    pass_on(0)
-    send_slot(3, 0)
     for j in range(layers):
         @pl.when(i * layers + j != me)
         def _():
@@ -291,13 +290,13 @@
     count = mats.shape[0] * mats.shape[1]
     matrices = mats[...].reshape(count, mats.shape[2])[:, :NBR * ORB]
     spread_q[...] = jnp.dot(matrices, pick_q[...], preferred_element_type=jnp.float32)
-    pass_on(1)
-    send_slot(4, 0)
+    pass_on(0)
+    send_slot(3, 0)
     spread_r[...] = jnp.dot(matrices, pick_r[...], preferred_element_type=jnp.float32)
     for copy in to_scalars:
         copy.wait()
-    pass_on(2)
-    send_slot(5, 0)
+    pass_on(1)
+    send_slot(4, 0)
 
     sub = lax.broadcasted_iota(jnp.int32, (8, WINDOW), 0)
     left_half = lax.broadcasted_iota(jnp.int32, (WINDOW, WINDOW), 1) < SPAN
@@ -340,7 +339,9 @@
                     rows += [q0 * rights[0], jnp.where(low_rows, q0, q1) * rights[1], q1 * rights[2]]
                 both[atom, four * 48:(four + 1) * 48, :] = jnp.concatenate(rows, axis=0).astype(jnp.bfloat16)
 
-        pl.when((h % 2 == 1) & (h < 6))(lambda: pass_on(lax.div(h, 2) + 3))
+
+        pl.when(lax.rem(h, 2) == 0)(lambda: pass_on(lax.div(h, 2) + 2))
+        pl.when(h == 0)(lambda: [send_slot(5, 0), None][1])
         return carry
 
     steps = mine * HALO // pair_of_atoms

time: 46.3 us -> 45.2 us (0.976)
  Pallas kernels: 44.8 us -> 43.7 us
    pallas_call x1, Pallas kernels: 40.5 us -> 39.4 us  [on_device(): pl.pallas_call(functools.partial(wire_kernel, inner, layers, side), out_s...]
where the time goes in v7:
time: 45.2 us; the launch traced here: 45.1 us
  Pallas kernels  43.7 us (97%)
  local copies, waits for them, and re-layouts  1.31 us (3%)
    pallas_call x1, Pallas kernels, on_device(): pl.pallas_call(functools.partial(wire_kernel, inner, layers, side), out_s...  39.4 us
    pallas_call x1, Pallas kernels, on_device(): pl.pallas_call(functools.partial(unpack_kernel, groups, per_dev), out_sha...  2.74 us
    pallas_call x1, Pallas kernels, on_device(): pl.pallas_call(functools.partial(pack_kernel, groups, per_dev), out_shape...  1.6 us
    unnamed x10, local copies, waits for them, and re-layouts  1.31 us

profile of v7, /device:TPU:0, one launch (start us, length us, event | category | flops | bytes accessed | tf_op | source)
XLA Modules:
  0.0 45.1 jit_solution(14653971198181158912)
XLA Ops:
  0.0 0.0 copy-start.4
  0.0 0.0 copy-start.3
  0.0 0.0 copy-start
  0.0 1.3 %copy-done = bf16[2,12,12,16,64]{4,3,2,1,0:T(8,128)(2,1)S(1)} copy-done((bf16[2,12,12,16,64]{4,3,2,1,0:T(8,128)(2,1)S(1)}, bf16[2,12,12,16,64]{4,3,2,1,0:T(8,128)(2,1)}, u32[]{:S(2)}) %copy-start) | copy-done | bytes 589848
  1.3 0.0 copy-start.1
  1.3 0.0 copy-start.2
  1.3 1.6 %shard_map.55.sent = bf16[16,16,1152]{2,1,0:T(8,128)(2,1)S(1)} custom-call(bf16[4608,64]{1,0:T(8,128)(2,1)S(1)} %bitcast.3), custom_call_target="tpu_custom_call" | custom-call | tf_op jit(solution)/shard_map/pallas_call | solution.py:453
  2.9 0.0 copy-done.4
  2.9 0.0 copy-done.3
  2.9 0.0 copy-done.1
  2.9 0.0 copy-done.2
  3.0 39.4 %shard_map.56.landed = bf16[16,16,1152]{2,1,0:T(8,128)(2,1)S(1)} custom-call(bf16[16,16,1152]{2,1,0:T(8,128)(2,1)S(1)} %shard_map.55.sent, bf16[12,12,64]{2,1,0:T(8,128)(2,1)S(1)} %bitcast.4, f32[9,1,64]{2,1,0:T(1,128)S(1)} %copy-done.2, s32[1,64]{1,0:T(1,128)S(1)} %copy-done.3, s32[1,64]{1,0:T(1,128)S(1)} %copy-done.4), custom_call_target="tpu_custom_call" | custom-call | tf_op jit(solution)/shard_map/pallas_call | solution.py:458
  42.3 2.7 %shard_map.57 = bf16[4608,64]{1,0:T(8,128)(2,1)} custom-call(bf16[16,16,1152]{2,1,0:T(8,128)(2,1)S(1)} %shard_map.56.landed), custom_call_target="tpu_custom_call" | custom-call | tf_op jit(solution)/shard_map/pallas_call | solution.py:491
Async XLA Ops:
  0.0 2.9 %copy-start.4 = (s32[1,64]{1,0:T(1,128)S(1)}, s32[1,64]{1,0:T(1,128)}, u32[]{:S(2)}) copy-start(s32[1,64]{1,0:T(1,128)} %shift_ref.1) | copy-start | bytes 772
  0.0 2.9 %copy-start.3 = (s32[1,64]{1,0:T(1,128)S(1)}, s32[1,64]{1,0:T(1,128)}, u32[]{:S(2)}) copy-start(s32[1,64]{1,0:T(1,128)} %near_ref.1) | copy-start | bytes 772
  0.0 1.3 %copy-start = (bf16[2,12,12,16,64]{4,3,2,1,0:T(8,128)(2,1)S(1)}, bf16[2,12,12,16,64]{4,3,2,1,0:T(8,128)(2,1)}, u32[]{:S(2)}) copy-start(bf16[2,12,12,16,64]{4,3,2,1,0:T(8,128)(2,1)} %param.5) | copy-start | bytes 1769476
  1.3 1.6 %copy-start.1 = (bf16[12,12,1,64]{3,1,2,0:T(8,128)(2,1)S(1)}, bf16[12,12,1,64]{3,1,2,0:T(8,128)(2,1)}, u32[]{:S(2)}) copy-start(bf16[12,12,1,64]{3,1,2,0:T(8,128)(2,1)} %param.6) | copy-start | bytes 55300
  1.3 1.6 %copy-start.2 = (f32[9,1,64]{2,1,0:T(1,128)S(1)}, f32[9,1,64]{2,1,0:T(1,128)}, u32[]{:S(2)}) copy-start(f32[9,1,64]{2,1,0:T(1,128)} %weight_ref.1) | copy-start | bytes 6916

commit v8 on v7

--- a/solution.py
+++ b/solution.py
@@ -71,12 +71,19 @@
     for g in range(groups):
         for j in range(wide.shape[0]):
             wide[j, g * local_e:(g + 1) * local_e, :] = landed[g, :, j * 128:(j + 1) * 128].astype(jnp.float32)
-    pick = order(groups, per_dev)
+    pick = order(per_dev, groups)
+    unit = eye(128)
     for e in range(local_e):
         rows = jnp.concatenate(
             [wide[j, pl.ds(e, groups, stride=local_e), :] for j in range(wide.shape[0])], axis=1)
         stack = jnp.concatenate([rows[:, i * BLOCK:(i + 1) * BLOCK] for i in range(per_dev)], axis=0)
-        turned = jnp.dot(stack.T.astype(jnp.bfloat16), pick, preferred_element_type=jnp.float32)
+        atoms = lax.dot_general(
+            pick, stack.astype(jnp.bfloat16), (((1,), (0,)), ((), ())), preferred_element_type=jnp.float32)
+        atoms = atoms.astype(jnp.bfloat16)
+        turned = jnp.concatenate([
+            lax.dot_general(
+                unit[:min(128, BLOCK - b), :min(128, BLOCK - b)], atoms[:, b:b + 128], NT,
+                preferred_element_type=jnp.float32) for b in range(0, BLOCK, 128)], axis=0)
         if lanes < 128:
             turned = jnp.concatenate([turned, jnp.zeros((BLOCK, 128 - lanes), jnp.float32)], axis=1)
         for j in range(tall.shape[0]):
@@ -391,8 +398,8 @@
                     green[later, partner], toeplitz[m * HALO * NBR + index], preferred_element_type=jnp.float32)
                 bands[a, k * PAIR:(k + 1) * PAIR, :] = banded.astype(jnp.bfloat16)
         parts = []
-        for a in range(HALO):
-            total = jnp.dot(both[m * HALO + a], bands[a], preferred_element_type=jnp.float32)
+        totals = [jnp.dot(both[m * HALO + a], bands[a], preferred_element_type=jnp.float32) for a in range(HALO)]
+        for total in totals:
             turned = lax.dot_general(unit, total.astype(jnp.bfloat16), NT, preferred_element_type=jnp.float32)
             parts += [turned[:SPAN], turned[SPAN:]]
         whole = jnp.concatenate(parts, axis=1)

time: 45.2 us -> 45.6 us (level)
    pallas_call x1, Pallas kernels: 2.74 us -> 4.76 us  [on_device(): pl.pallas_call(functools.partial(unpack_kernel, groups, per_dev), out_sha...]
    pallas_call x1, Pallas kernels: 39.4 us -> 37.7 us  [on_device(): pl.pallas_call(functools.partial(wire_kernel, inner, layers, side), out_s...]
where the time goes in v8:
time: 45.6 us; the launch traced here: 45.4 us
  Pallas kernels  44.1 us (97%)
  local copies, waits for them, and re-layouts  1.31 us (3%)
    pallas_call x1, Pallas kernels, on_device(): pl.pallas_call(functools.partial(wire_kernel, inner, layers, side), out_s...  37.7 us
    pallas_call x1, Pallas kernels, on_device(): pl.pallas_call(functools.partial(unpack_kernel, groups, per_dev), out_sha...  4.76 us
    pallas_call x1, Pallas kernels, on_device(): pl.pallas_call(functools.partial(pack_kernel, groups, per_dev), out_shape...  1.6 us
    unnamed x10, local copies, waits for them, and re-layouts  1.31 us

profile of v8, /device:TPU:0, one launch (start us, length us, event | category | flops | bytes accessed | tf_op | source)
XLA Modules:
  0.0 45.4 jit_solution(2013355724567141841)
XLA Ops:
  0.0 0.0 copy-start.4
  0.0 0.0 copy-start.3
  0.0 0.0 copy-start
  0.0 1.3 %copy-done = bf16[2,12,12,16,64]{4,3,2,1,0:T(8,128)(2,1)S(1)} copy-done((bf16[2,12,12,16,64]{4,3,2,1,0:T(8,128)(2,1)S(1)}, bf16[2,12,12,16,64]{4,3,2,1,0:T(8,128)(2,1)}, u32[]{:S(2)}) %copy-start) | copy-done | bytes 589848
  1.3 0.0 copy-start.1
  1.3 0.0 copy-start.2
  1.3 1.6 %shard_map.55.sent = bf16[16,16,1152]{2,1,0:T(8,128)(2,1)S(1)} custom-call(bf16[4608,64]{1,0:T(8,128)(2,1)S(1)} %bitcast.3), custom_call_target="tpu_custom_call" | custom-call | tf_op jit(solution)/shard_map/pallas_call | solution.py:460
  2.9 0.0 copy-done.4
  2.9 0.0 copy-done.3
  2.9 0.0 copy-done.1
  2.9 0.0 copy-done.2
  3.0 37.7 %shard_map.56.landed = bf16[16,16,1152]{2,1,0:T(8,128)(2,1)S(1)} custom-call(bf16[16,16,1152]{2,1,0:T(8,128)(2,1)S(1)} %shard_map.55.sent, bf16[12,12,64]{2,1,0:T(8,128)(2,1)S(1)} %bitcast.4, f32[9,1,64]{2,1,0:T(1,128)S(1)} %copy-done.2, s32[1,64]{1,0:T(1,128)S(1)} %copy-done.3, s32[1,64]{1,0:T(1,128)S(1)} %copy-done.4), custom_call_target="tpu_custom_call" | custom-call | tf_op jit(solution)/shard_map/pallas_call | solution.py:465
  40.6 4.8 %shard_map.57 = bf16[4608,64]{1,0:T(8,128)(2,1)} custom-call(bf16[16,16,1152]{2,1,0:T(8,128)(2,1)S(1)} %shard_map.56.landed), custom_call_target="tpu_custom_call" | custom-call | tf_op jit(solution)/shard_map/pallas_call | solution.py:498
Async XLA Ops:
  0.0 2.9 %copy-start.4 = (s32[1,64]{1,0:T(1,128)S(1)}, s32[1,64]{1,0:T(1,128)}, u32[]{:S(2)}) copy-start(s32[1,64]{1,0:T(1,128)} %shift_ref.1) | copy-start | bytes 772
  0.0 2.9 %copy-start.3 = (s32[1,64]{1,0:T(1,128)S(1)}, s32[1,64]{1,0:T(1,128)}, u32[]{:S(2)}) copy-start(s32[1,64]{1,0:T(1,128)} %near_ref.1) | copy-start | bytes 772
  0.0 1.3 %copy-start = (bf16[2,12,12,16,64]{4,3,2,1,0:T(8,128)(2,1)S(1)}, bf16[2,12,12,16,64]{4,3,2,1,0:T(8,128)(2,1)}, u32[]{:S(2)}) copy-start(bf16[2,12,12,16,64]{4,3,2,1,0:T(8,128)(2,1)} %param.5) | copy-start | bytes 1769476
  1.3 1.6 %copy-start.1 = (bf16[12,12,1,64]{3,1,2,0:T(8,128)(2,1)S(1)}, bf16[12,12,1,64]{3,1,2,0:T(8,128)(2,1)}, u32[]{:S(2)}) copy-start(bf16[12,12,1,64]{3,1,2,0:T(8,128)(2,1)} %param.6) | copy-start | bytes 55300
  1.3 1.6 %copy-start.2 = (f32[9,1,64]{2,1,0:T(1,128)S(1)}, f32[9,1,64]{2,1,0:T(1,128)}, u32[]{:S(2)}) copy-start(f32[9,1,64]{2,1,0:T(1,128)} %weight_ref.1) | copy-start | bytes 6916

commit v9 on v7

--- a/solution.py
+++ b/solution.py
@@ -76,7 +76,7 @@
         rows = jnp.concatenate(
             [wide[j, pl.ds(e, groups, stride=local_e), :] for j in range(wide.shape[0])], axis=1)
         stack = jnp.concatenate([rows[:, i * BLOCK:(i + 1) * BLOCK] for i in range(per_dev)], axis=0)
-        turned = jnp.dot(stack.T.astype(jnp.bfloat16), pick, preferred_element_type=jnp.float32)
+        turned = jnp.dot(stack.astype(jnp.bfloat16).T, pick, preferred_element_type=jnp.float32)
         if lanes < 128:
             turned = jnp.concatenate([turned, jnp.zeros((BLOCK, 128 - lanes), jnp.float32)], axis=1)
         for j in range(tall.shape[0]):
@@ -158,30 +158,6 @@
     weight_rows[:BAND, :] = weight_ref[:, 0, :]
     table_tall(padded, weight_rows, mats_in)
 
-    landed[pl.ds(1, mine), side + i] = sent[pl.ds(i * mine, mine)]
-
-    @pl.when(i > 0)
-    def _():
-        landed[0, side + i] = sent[lax.rem(i * mine - 1 + chunks, chunks)]
-
-    @pl.when(i < inner - 1)
-    def _():
-        landed[slots - 1, side + i] = sent[lax.rem(i * mine + mine, chunks)]
-
-    @pl.when(first & jnp.logical_not(slab_below))
-    def _():
-        landed[0, side:side + inner] = jnp.zeros((inner, local_e, width), landed.dtype)
-
-    @pl.when(last & jnp.logical_not(slab_above))
-    def _():
-        landed[slots - 1, side:side + inner] = jnp.zeros((inner, local_e, width), landed.dtype)
-
-    def clear(start):
-        landed[:, start:start + side] = jnp.zeros((slots, side, local_e, width), landed.dtype)
-
-    pl.when(jnp.logical_not(below))(lambda: clear(0))
-    pl.when(jnp.logical_not(above))(lambda: clear(side + inner))
-
     tables = ((mats_in, mats), (near_ref, near), (shift_ref, shifts))
 
     @pl.when(owner == i)
@@ -240,6 +216,30 @@
                 table(number, j, spot, to).start()
 
     lax.fori_loop(0, 3, send_slot, 0)
+
+    landed[pl.ds(1, mine), side + i] = sent[pl.ds(i * mine, mine)]
+
+    @pl.when(i > 0)
+    def _():
+        landed[0, side + i] = sent[lax.rem(i * mine - 1 + chunks, chunks)]
+
+    @pl.when(i < inner - 1)
+    def _():
+        landed[slots - 1, side + i] = sent[lax.rem(i * mine + mine, chunks)]
+
+    @pl.when(first & jnp.logical_not(slab_below))
+    def _():
+        landed[0, side:side + inner] = jnp.zeros((inner, local_e, width), landed.dtype)
+
+    @pl.when(last & jnp.logical_not(slab_above))
+    def _():
+        landed[slots - 1, side:side + inner] = jnp.zeros((inner, local_e, width), landed.dtype)
+
+    def clear(start):
+        landed[:, start:start + side] = jnp.zeros((slots, side, local_e, width), landed.dtype)
+
+    pl.when(jnp.logical_not(below))(lambda: clear(0))
+    pl.when(jnp.logical_not(above))(lambda: clear(side + inner))
 
     wide = NBR * PAIR
     lane = lax.broadcasted_iota(jnp.int32, (8, wide), 1)
@@ -391,8 +391,8 @@
                     green[later, partner], toeplitz[m * HALO * NBR + index], preferred_element_type=jnp.float32)
                 bands[a, k * PAIR:(k + 1) * PAIR, :] = banded.astype(jnp.bfloat16)
         parts = []
-        for a in range(HALO):
-            total = jnp.dot(both[m * HALO + a], bands[a], preferred_element_type=jnp.float32)
+        totals = [jnp.dot(both[m * HALO + a], bands[a], preferred_element_type=jnp.float32) for a in range(HALO)]
+        for total in totals:
             turned = lax.dot_general(unit, total.astype(jnp.bfloat16), NT, preferred_element_type=jnp.float32)
             parts += [turned[:SPAN], turned[SPAN:]]
         whole = jnp.concatenate(parts, axis=1)

time: 45.2 us -> 43.4 us (0.960)
  Pallas kernels: 43.7 us -> 41.9 us
    pallas_call x1, Pallas kernels: 39.4 us -> 37.7 us  [on_device(): pl.pallas_call(functools.partial(wire_kernel, inner, layers, side), out_s...]
where the time goes in v9:
time: 43.4 us; the launch traced here: 43.3 us
  Pallas kernels  41.9 us (97%)
  local copies, waits for them, and re-layouts  1.31 us (3%)
    pallas_call x1, Pallas kernels, on_device(): pl.pallas_call(functools.partial(wire_kernel, inner, layers, side), out_s...  37.7 us
    pallas_call x1, Pallas kernels, on_device(): pl.pallas_call(functools.partial(unpack_kernel, groups, per_dev), out_sha...  2.64 us
    pallas_call x1, Pallas kernels, on_device(): pl.pallas_call(functools.partial(pack_kernel, groups, per_dev), out_shape...  1.6 us
    unnamed x10, local copies, waits for them, and re-layouts  1.31 us

profile of v9, /device:TPU:0, one launch (start us, length us, event | category | flops | bytes accessed | tf_op | source)
XLA Modules:
  0.0 43.3 jit_solution(10817662786522144079)
XLA Ops:
  0.0 0.0 copy-start.4
  0.0 0.0 copy-start.3
  0.0 0.0 copy-start
  0.0 1.3 %copy-done = bf16[2,12,12,16,64]{4,3,2,1,0:T(8,128)(2,1)S(1)} copy-done((bf16[2,12,12,16,64]{4,3,2,1,0:T(8,128)(2,1)S(1)}, bf16[2,12,12,16,64]{4,3,2,1,0:T(8,128)(2,1)}, u32[]{:S(2)}) %copy-start) | copy-done | bytes 589848
  1.3 0.0 copy-start.1
  1.3 0.0 copy-start.2
  1.3 1.6 %shard_map.55.sent = bf16[16,16,1152]{2,1,0:T(8,128)(2,1)S(1)} custom-call(bf16[4608,64]{1,0:T(8,128)(2,1)S(1)} %bitcast.3), custom_call_target="tpu_custom_call" | custom-call | tf_op jit(solution)/shard_map/pallas_call | solution.py:453
  2.9 0.0 copy-done.4
  2.9 0.0 copy-done.3
  2.9 0.0 copy-done.1
  2.9 0.0 copy-done.2
  3.0 37.7 %shard_map.56.landed = bf16[16,16,1152]{2,1,0:T(8,128)(2,1)S(1)} custom-call(bf16[16,16,1152]{2,1,0:T(8,128)(2,1)S(1)} %shard_map.55.sent, bf16[12,12,64]{2,1,0:T(8,128)(2,1)S(1)} %bitcast.4, f32[9,1,64]{2,1,0:T(1,128)S(1)} %copy-done.2, s32[1,64]{1,0:T(1,128)S(1)} %copy-done.3, s32[1,64]{1,0:T(1,128)S(1)} %copy-done.4), custom_call_target="tpu_custom_call" | custom-call | tf_op jit(solution)/shard_map/pallas_call | solution.py:458
  40.6 2.6 %shard_map.57 = bf16[4608,64]{1,0:T(8,128)(2,1)} custom-call(bf16[16,16,1152]{2,1,0:T(8,128)(2,1)S(1)} %shard_map.56.landed), custom_call_target="tpu_custom_call" | custom-call | tf_op jit(solution)/shard_map/pallas_call | solution.py:491
Async XLA Ops:
  0.0 2.9 %copy-start.4 = (s32[1,64]{1,0:T(1,128)S(1)}, s32[1,64]{1,0:T(1,128)}, u32[]{:S(2)}) copy-start(s32[1,64]{1,0:T(1,128)} %shift_ref.1) | copy-start | bytes 772
  0.0 2.9 %copy-start.3 = (s32[1,64]{1,0:T(1,128)S(1)}, s32[1,64]{1,0:T(1,128)}, u32[]{:S(2)}) copy-start(s32[1,64]{1,0:T(1,128)} %near_ref.1) | copy-start | bytes 772
  0.0 1.3 %copy-start = (bf16[2,12,12,16,64]{4,3,2,1,0:T(8,128)(2,1)S(1)}, bf16[2,12,12,16,64]{4,3,2,1,0:T(8,128)(2,1)}, u32[]{:S(2)}) copy-start(bf16[2,12,12,16,64]{4,3,2,1,0:T(8,128)(2,1)} %param.5) | copy-start | bytes 1769476
  1.3 1.6 %copy-start.1 = (bf16[12,12,1,64]{3,1,2,0:T(8,128)(2,1)S(1)}, bf16[12,12,1,64]{3,1,2,0:T(8,128)(2,1)}, u32[]{:S(2)}) copy-start(bf16[12,12,1,64]{3,1,2,0:T(8,128)(2,1)} %param.6) | copy-start | bytes 55300
  1.3 1.6 %copy-start.2 = (f32[9,1,64]{2,1,0:T(1,128)S(1)}, f32[9,1,64]{2,1,0:T(1,128)}, u32[]{:S(2)}) copy-start(f32[9,1,64]{2,1,0:T(1,128)} %weight_ref.1) | copy-start | bytes 6916

commit v10 on v9

--- a/solution.py
+++ b/solution.py
@@ -301,7 +301,7 @@
     sub = lax.broadcasted_iota(jnp.int32, (8, WINDOW), 0)
     left_half = lax.broadcasted_iota(jnp.int32, (WINDOW, WINDOW), 1) < SPAN
     low_rows = lax.broadcasted_iota(jnp.int32, (8, wide), 0) < 4
-    pair_of_atoms = 2
+    batch = HALO
     zero = jnp.zeros((16, WINDOW), jnp.bfloat16)
 
     def window_of(m, index):
@@ -309,25 +309,26 @@
         return shift, jnp.where(shift >= 0, 1, 0)
 
     def prepare(h, carry):
-        m = lax.div(h, HALO // pair_of_atoms)
-        for a in range(pair_of_atoms):
-            atom = h * pair_of_atoms + a
-            tiles = []
-            for k in range(NBR):
-                index = lax.rem(atom, HALO) * NBR + k
-                shift, later = window_of(m, index)
-                base = shift + side * local_e - BAND // 2 - later * late
-                weight = weights[m, pl.ds(index, 1), :]
-                tiles.append(pltpu.roll(jnp.broadcast_to(weight, (8, WINDOW)), WINDOW - BAND + 1 - base, 1))
-            for step in (1, 2, 4):
-                tiles = [jnp.where((sub & step) != 0, pltpu.roll(tile, step, 1), tile) for tile in tiles]
-            tiles = [jnp.concatenate([tile, pltpu.roll(tile, 8, 1)], axis=0).astype(jnp.bfloat16) for tile in tiles]
-            for b in range(WINDOW // 16):
-                for k in range(NBR):
-                    tile = pltpu.roll(tiles[k], 16 * b, 1) if b else tiles[k]
-                    toeplitz[atom * NBR + k, 16 * b:16 * b + 16] = jnp.where(left_half[:16], tile, zero)
-                    low = WINDOW + (16 * b - SPAN) % WINDOW
-                    toeplitz[atom * NBR + k, low:low + 16] = jnp.where(left_half[:16], zero, tile)
+        m = lax.div(h, HALO // batch)
+        tiles = []
+        first_pair = h * batch * NBR
+        for k in range(batch * NBR):
+            index = lax.rem(h * batch, HALO) * NBR + k
+            shift, later = window_of(m, index)
+            base = shift + side * local_e - BAND // 2 - later * late
+            weight = weights[m, pl.ds(index, 1), :]
+            tiles.append(pltpu.roll(jnp.broadcast_to(weight, (8, WINDOW)), WINDOW - BAND + 1 - base, 1))
+        for step in (1, 2, 4):
+            tiles = [jnp.where((sub & step) != 0, pltpu.roll(tile, step, 1), tile) for tile in tiles]
+        tiles = [jnp.concatenate([tile, pltpu.roll(tile, 8, 1)], axis=0).astype(jnp.bfloat16) for tile in tiles]
+        for b in range(WINDOW // 16):
+            for k in range(batch * NBR):
+                tile = pltpu.roll(tiles[k], 16 * b, 1) if b else tiles[k]
+                toeplitz[first_pair + k, 16 * b:16 * b + 16] = jnp.where(left_half[:16], tile, zero)
+                low = WINDOW + (16 * b - SPAN) % WINDOW
+                toeplitz[first_pair + k, low:low + 16] = jnp.where(left_half[:16], zero, tile)
+        for a in range(batch):
+            atom = h * batch + a
             right = spread_r[pl.ds(pl.multiple_of(atom * 16, 16), 16), :]
             rights = (right[:8], jnp.concatenate([right[8:12], right[:4]], axis=0), right[4:12])
             for four in range(ORB // 4):
@@ -340,12 +341,12 @@
                 both[atom, four * 48:(four + 1) * 48, :] = jnp.concatenate(rows, axis=0).astype(jnp.bfloat16)
 
 
-        pl.when(lax.rem(h, 2) == 0)(lambda: pass_on(lax.div(h, 2) + 2))
+        pass_on(h + 2)
         pl.when(h == 0)(lambda: [send_slot(5, 0), None][1])
         return carry
 
-    steps = mine * HALO // pair_of_atoms
-    assert slots == 6 and steps >= slots
+    steps = mine * HALO // batch
+    assert steps == slots - 2
     lax.fori_loop(0, steps, prepare, 0)
 
     unit = eye(128)

time: 43.4 us -> 41.4 us (0.954)
  Pallas kernels: 41.9 us -> 39.9 us
    pallas_call x1, Pallas kernels: 37.7 us -> 35.7 us  [on_device(): pl.pallas_call(functools.partial(wire_kernel, inner, layers, side), out_s...]
where the time goes in v10:
time: 41.4 us; the launch traced here: 41.2 us
  Pallas kernels  39.9 us (96%)
  local copies, waits for them, and re-layouts  1.31 us (3%)
    pallas_call x1, Pallas kernels, on_device(): pl.pallas_call(functools.partial(wire_kernel, inner, layers, side), out_s...  35.7 us
    pallas_call x1, Pallas kernels, on_device(): pl.pallas_call(functools.partial(unpack_kernel, groups, per_dev), out_sha...  2.64 us
    pallas_call x1, Pallas kernels, on_device(): pl.pallas_call(functools.partial(pack_kernel, groups, per_dev), out_shape...  1.6 us
    unnamed x10, local copies, waits for them, and re-layouts  1.31 us

profile of v10, /device:TPU:0, one launch (start us, length us, event | category | flops | bytes accessed | tf_op | source)
XLA Modules:
  0.0 41.2 jit_solution(2466107266549096122)
XLA Ops:
  0.0 0.0 copy-start.4
  0.0 0.0 copy-start.3
  0.0 0.0 copy-start
  0.0 1.3 %copy-done = bf16[2,12,12,16,64]{4,3,2,1,0:T(8,128)(2,1)S(1)} copy-done((bf16[2,12,12,16,64]{4,3,2,1,0:T(8,128)(2,1)S(1)}, bf16[2,12,12,16,64]{4,3,2,1,0:T(8,128)(2,1)}, u32[]{:S(2)}) %copy-start) | copy-done | bytes 589848
  1.3 0.0 copy-start.1
  1.3 0.0 copy-start.2
  1.3 1.6 %shard_map.55.sent = bf16[16,16,1152]{2,1,0:T(8,128)(2,1)S(1)} custom-call(bf16[4608,64]{1,0:T(8,128)(2,1)S(1)} %bitcast.3), custom_call_target="tpu_custom_call" | custom-call | tf_op jit(solution)/shard_map/pallas_call | solution.py:454
  2.9 0.0 copy-done.4
  2.9 0.0 copy-done.3
  2.9 0.0 copy-done.1
  2.9 0.0 copy-done.2
  3.0 35.7 %shard_map.56.landed = bf16[16,16,1152]{2,1,0:T(8,128)(2,1)S(1)} custom-call(bf16[16,16,1152]{2,1,0:T(8,128)(2,1)S(1)} %shard_map.55.sent, bf16[12,12,64]{2,1,0:T(8,128)(2,1)S(1)} %bitcast.4, f32[9,1,64]{2,1,0:T(1,128)S(1)} %copy-done.2, s32[1,64]{1,0:T(1,128)S(1)} %copy-done.3, s32[1,64]{1,0:T(1,128)S(1)} %copy-done.4), custom_call_target="tpu_custom_call" | custom-call | tf_op jit(solution)/shard_map/pallas_call | solution.py:459
  38.6 2.6 %shard_map.57 = bf16[4608,64]{1,0:T(8,128)(2,1)} custom-call(bf16[16,16,1152]{2,1,0:T(8,128)(2,1)S(1)} %shard_map.56.landed), custom_call_target="tpu_custom_call" | custom-call | tf_op jit(solution)/shard_map/pallas_call | solution.py:492
Async XLA Ops:
  0.0 2.9 %copy-start.4 = (s32[1,64]{1,0:T(1,128)S(1)}, s32[1,64]{1,0:T(1,128)}, u32[]{:S(2)}) copy-start(s32[1,64]{1,0:T(1,128)} %shift_ref.1) | copy-start | bytes 772
  0.0 2.9 %copy-start.3 = (s32[1,64]{1,0:T(1,128)S(1)}, s32[1,64]{1,0:T(1,128)}, u32[]{:S(2)}) copy-start(s32[1,64]{1,0:T(1,128)} %near_ref.1) | copy-start | bytes 772
  0.0 1.3 %copy-start = (bf16[2,12,12,16,64]{4,3,2,1,0:T(8,128)(2,1)S(1)}, bf16[2,12,12,16,64]{4,3,2,1,0:T(8,128)(2,1)}, u32[]{:S(2)}) copy-start(bf16[2,12,12,16,64]{4,3,2,1,0:T(8,128)(2,1)} %param.5) | copy-start | bytes 1769476
  1.3 1.6 %copy-start.1 = (bf16[12,12,1,64]{3,1,2,0:T(8,128)(2,1)S(1)}, bf16[12,12,1,64]{3,1,2,0:T(8,128)(2,1)}, u32[]{:S(2)}) copy-start(bf16[12,12,1,64]{3,1,2,0:T(8,128)(2,1)} %param.6) | copy-start | bytes 55300
  1.3 1.6 %copy-start.2 = (f32[9,1,64]{2,1,0:T(1,128)S(1)}, f32[9,1,64]{2,1,0:T(1,128)}, u32[]{:S(2)}) copy-start(f32[9,1,64]{2,1,0:T(1,128)} %weight_ref.1) | copy-start | bytes 6916

commit v11 on v10

--- a/solution.py
+++ b/solution.py
@@ -72,15 +72,20 @@
         for j in range(wide.shape[0]):
             wide[j, g * local_e:(g + 1) * local_e, :] = landed[g, :, j * 128:(j + 1) * 128].astype(jnp.float32)
     pick = order(groups, per_dev)
-    for e in range(local_e):
-        rows = jnp.concatenate(
-            [wide[j, pl.ds(e, groups, stride=local_e), :] for j in range(wide.shape[0])], axis=1)
-        stack = jnp.concatenate([rows[:, i * BLOCK:(i + 1) * BLOCK] for i in range(per_dev)], axis=0)
-        turned = jnp.dot(stack.astype(jnp.bfloat16).T, pick, preferred_element_type=jnp.float32)
-        if lanes < 128:
-            turned = jnp.concatenate([turned, jnp.zeros((BLOCK, 128 - lanes), jnp.float32)], axis=1)
-        for j in range(tall.shape[0]):
-            tall[j, pl.ds(e, BLOCK, stride=local_e), :] = turned[:, j * 128:(j + 1) * 128]
+    some = min(4, local_e)
+    for start in range(0, local_e, some):
+        stacks = []
+        for e in range(start, start + some):
+            rows = jnp.concatenate(
+                [wide[j, pl.ds(e, groups, stride=local_e), :] for j in range(wide.shape[0])], axis=1)
+            stacks.append(jnp.concatenate(
+                [rows[:, i * BLOCK:(i + 1) * BLOCK] for i in range(per_dev)], axis=0).astype(jnp.bfloat16))
+        turns = [jnp.dot(stack.T, pick, preferred_element_type=jnp.float32) for stack in stacks]
+        for e, turned in zip(range(start, start + some), turns):
+            if lanes < 128:
+                turned = jnp.concatenate([turned, jnp.zeros((BLOCK, 128 - lanes), jnp.float32)], axis=1)
+            for j in range(tall.shape[0]):
+                tall[j, pl.ds(e, BLOCK, stride=local_e), :] = turned[:, j * 128:(j + 1) * 128]
     for j in range(tall.shape[0]):
         out_ref[:, j * 128:j * 128 + lanes] = tall[j, :out_ref.shape[0], :lanes].astype(jnp.bfloat16)
 
@@ -395,10 +400,11 @@
         totals = [jnp.dot(both[m * HALO + a], bands[a], preferred_element_type=jnp.float32) for a in range(HALO)]
         for total in totals:
             turned = lax.dot_general(unit, total.astype(jnp.bfloat16), NT, preferred_element_type=jnp.float32)
+            turned = turned.astype(jnp.bfloat16)
             parts += [turned[:SPAN], turned[SPAN:]]
         whole = jnp.concatenate(parts, axis=1)
         for d in range(inner):
-            out_ref[d, m] = whole[d * local_e:(d + 1) * local_e].astype(jnp.bfloat16)
+            out_ref[d, m] = whole[d * local_e:(d + 1) * local_e]
         for step in range(1, inner):
             share(step, m, i).start()
         back_ref[i * mine + m] = out_ref[i, m]

time: 41.4 us -> 41.4 us (level)
  no operation moved by 1% of the time
where the time goes in v11:
time: 41.4 us; the launch traced here: 41.3 us
  Pallas kernels  39.9 us (96%)
  local copies, waits for them, and re-layouts  1.31 us (3%)
    pallas_call x1, Pallas kernels, on_device(): pl.pallas_call(functools.partial(wire_kernel, inner, layers, side), out_s...  35.6 us
    pallas_call x1, Pallas kernels, on_device(): pl.pallas_call(functools.partial(unpack_kernel, groups, per_dev), out_sha...  2.68 us
    pallas_call x1, Pallas kernels, on_device(): pl.pallas_call(functools.partial(pack_kernel, groups, per_dev), out_shape...  1.6 us
    unnamed x10, local copies, waits for them, and re-layouts  1.31 us

profile of v11, /device:TPU:0, one launch (start us, length us, event | category | flops | bytes accessed | tf_op | source)
XLA Modules:
  0.0 41.3 jit_solution(3685551586727039332)
XLA Ops:
  0.0 0.0 copy-start.4
  0.0 0.0 copy-start.3
  0.0 0.0 copy-start
  0.0 1.3 %copy-done = bf16[2,12,12,16,64]{4,3,2,1,0:T(8,128)(2,1)S(1)} copy-done((bf16[2,12,12,16,64]{4,3,2,1,0:T(8,128)(2,1)S(1)}, bf16[2,12,12,16,64]{4,3,2,1,0:T(8,128)(2,1)}, u32[]{:S(2)}) %copy-start) | copy-done | bytes 589848
  1.3 0.0 copy-start.1
  1.3 0.0 copy-start.2
  1.3 1.6 %shard_map.55.sent = bf16[16,16,1152]{2,1,0:T(8,128)(2,1)S(1)} custom-call(bf16[4608,64]{1,0:T(8,128)(2,1)S(1)} %bitcast.3), custom_call_target="tpu_custom_call" | custom-call | tf_op jit(solution)/shard_map/pallas_call | solution.py:460
  2.9 0.0 copy-done.4
  2.9 0.0 copy-done.3
  2.9 0.0 copy-done.1
  2.9 0.0 copy-done.2
  3.0 35.6 %shard_map.56.landed = bf16[16,16,1152]{2,1,0:T(8,128)(2,1)S(1)} custom-call(bf16[16,16,1152]{2,1,0:T(8,128)(2,1)S(1)} %shard_map.55.sent, bf16[12,12,64]{2,1,0:T(8,128)(2,1)S(1)} %bitcast.4, f32[9,1,64]{2,1,0:T(1,128)S(1)} %copy-done.2, s32[1,64]{1,0:T(1,128)S(1)} %copy-done.3, s32[1,64]{1,0:T(1,128)S(1)} %copy-done.4), custom_call_target="tpu_custom_call" | custom-call | tf_op jit(solution)/shard_map/pallas_call | solution.py:465
  38.6 2.7 %shard_map.57 = bf16[4608,64]{1,0:T(8,128)(2,1)} custom-call(bf16[16,16,1152]{2,1,0:T(8,128)(2,1)S(1)} %shard_map.56.landed), custom_call_target="tpu_custom_call" | custom-call | tf_op jit(solution)/shard_map/pallas_call | solution.py:498
Async XLA Ops:
  0.0 2.9 %copy-start.4 = (s32[1,64]{1,0:T(1,128)S(1)}, s32[1,64]{1,0:T(1,128)}, u32[]{:S(2)}) copy-start(s32[1,64]{1,0:T(1,128)} %shift_ref.1) | copy-start | bytes 772
  0.0 2.9 %copy-start.3 = (s32[1,64]{1,0:T(1,128)S(1)}, s32[1,64]{1,0:T(1,128)}, u32[]{:S(2)}) copy-start(s32[1,64]{1,0:T(1,128)} %near_ref.1) | copy-start | bytes 772
  0.0 1.3 %copy-start = (bf16[2,12,12,16,64]{4,3,2,1,0:T(8,128)(2,1)S(1)}, bf16[2,12,12,16,64]{4,3,2,1,0:T(8,128)(2,1)}, u32[]{:S(2)}) copy-start(bf16[2,12,12,16,64]{4,3,2,1,0:T(8,128)(2,1)} %param.5) | copy-start | bytes 1769476
  1.3 1.6 %copy-start.1 = (bf16[12,12,1,64]{3,1,2,0:T(8,128)(2,1)S(1)}, bf16[12,12,1,64]{3,1,2,0:T(8,128)(2,1)}, u32[]{:S(2)}) copy-start(bf16[12,12,1,64]{3,1,2,0:T(8,128)(2,1)} %param.6) | copy-start | bytes 55300
  1.3 1.6 %copy-start.2 = (f32[9,1,64]{2,1,0:T(1,128)S(1)}, f32[9,1,64]{2,1,0:T(1,128)}, u32[]{:S(2)}) copy-start(f32[9,1,64]{2,1,0:T(1,128)} %weight_ref.1) | copy-start | bytes 6916

commit v12 on v11

--- a/solution.py
+++ b/solution.py
@@ -388,6 +388,7 @@
 
     def chunk(m, carry):
         turn(m + 2, 0)
+        totals = []
         for a in range(HALO):
             for k in range(NBR):
                 index = a * NBR + k
@@ -396,8 +397,9 @@
                 banded = jnp.dot(
                     green[later, partner], toeplitz[m * HALO * NBR + index], preferred_element_type=jnp.float32)
                 bands[a, k * PAIR:(k + 1) * PAIR, :] = banded.astype(jnp.bfloat16)
+            if a % 2:
+                totals += [jnp.dot(both[m * HALO + b], bands[b], preferred_element_type=jnp.float32) for b in (a - 1, a)]
         parts = []
-        totals = [jnp.dot(both[m * HALO + a], bands[a], preferred_element_type=jnp.float32) for a in range(HALO)]
         for total in totals:
             turned = lax.dot_general(unit, total.astype(jnp.bfloat16), NT, preferred_element_type=jnp.float32)
             turned = turned.astype(jnp.bfloat16)

time: 41.4 us -> 41.4 us (level)
  no operation moved by 1% of the time
where the time goes in v12:
time: 41.4 us; the launch traced here: 41.2 us
  Pallas kernels  39.9 us (96%)
  local copies, waits for them, and re-layouts  1.31 us (3%)
    pallas_call x1, Pallas kernels, on_device(): pl.pallas_call(functools.partial(wire_kernel, inner, layers, side), out_s...  35.6 us
    pallas_call x1, Pallas kernels, on_device(): pl.pallas_call(functools.partial(unpack_kernel, groups, per_dev), out_sha...  2.68 us
    pallas_call x1, Pallas kernels, on_device(): pl.pallas_call(functools.partial(pack_kernel, groups, per_dev), out_shape...  1.6 us
    unnamed x10, local copies, waits for them, and re-layouts  1.31 us

profile of v12, /device:TPU:0, one launch (start us, length us, event | category | flops | bytes accessed | tf_op | source)
XLA Modules:
  0.0 41.2 jit_solution(15037806790010786176)
XLA Ops:
  0.0 0.0 copy-start.4
  0.0 0.0 copy-start.3
  0.0 0.0 copy-start
  0.0 1.3 %copy-done = bf16[2,12,12,16,64]{4,3,2,1,0:T(8,128)(2,1)S(1)} copy-done((bf16[2,12,12,16,64]{4,3,2,1,0:T(8,128)(2,1)S(1)}, bf16[2,12,12,16,64]{4,3,2,1,0:T(8,128)(2,1)}, u32[]{:S(2)}) %copy-start) | copy-done | bytes 589848
  1.3 0.0 copy-start.1
  1.3 0.0 copy-start.2
  1.3 1.6 %shard_map.55.sent = bf16[16,16,1152]{2,1,0:T(8,128)(2,1)S(1)} custom-call(bf16[4608,64]{1,0:T(8,128)(2,1)S(1)} %bitcast.3), custom_call_target="tpu_custom_call" | custom-call | tf_op jit(solution)/shard_map/pallas_call | solution.py:462
  2.9 0.0 copy-done.4
  2.9 0.0 copy-done.3
  2.9 0.0 copy-done.1
  2.9 0.0 copy-done.2
  3.0 35.6 %shard_map.56.landed = bf16[16,16,1152]{2,1,0:T(8,128)(2,1)S(1)} custom-call(bf16[16,16,1152]{2,1,0:T(8,128)(2,1)S(1)} %shard_map.55.sent, bf16[12,12,64]{2,1,0:T(8,128)(2,1)S(1)} %bitcast.4, f32[9,1,64]{2,1,0:T(1,128)S(1)} %copy-done.2, s32[1,64]{1,0:T(1,128)S(1)} %copy-done.3, s32[1,64]{1,0:T(1,128)S(1)} %copy-done.4), custom_call_target="tpu_custom_call" | custom-call | tf_op jit(solution)/shard_map/pallas_call | solution.py:467
  38.6 2.7 %shard_map.57 = bf16[4608,64]{1,0:T(8,128)(2,1)} custom-call(bf16[16,16,1152]{2,1,0:T(8,128)(2,1)S(1)} %shard_map.56.landed), custom_call_target="tpu_custom_call" | custom-call | tf_op jit(solution)/shard_map/pallas_call | solution.py:500
Async XLA Ops:
  0.0 2.9 %copy-start.4 = (s32[1,64]{1,0:T(1,128)S(1)}, s32[1,64]{1,0:T(1,128)}, u32[]{:S(2)}) copy-start(s32[1,64]{1,0:T(1,128)} %shift_ref.1) | copy-start | bytes 772
  0.0 2.9 %copy-start.3 = (s32[1,64]{1,0:T(1,128)S(1)}, s32[1,64]{1,0:T(1,128)}, u32[]{:S(2)}) copy-start(s32[1,64]{1,0:T(1,128)} %near_ref.1) | copy-start | bytes 772
  0.0 1.3 %copy-start = (bf16[2,12,12,16,64]{4,3,2,1,0:T(8,128)(2,1)S(1)}, bf16[2,12,12,16,64]{4,3,2,1,0:T(8,128)(2,1)}, u32[]{:S(2)}) copy-start(bf16[2,12,12,16,64]{4,3,2,1,0:T(8,128)(2,1)} %param.5) | copy-start | bytes 1769476
  1.3 1.6 %copy-start.1 = (bf16[12,12,1,64]{3,1,2,0:T(8,128)(2,1)S(1)}, bf16[12,12,1,64]{3,1,2,0:T(8,128)(2,1)}, u32[]{:S(2)}) copy-start(bf16[12,12,1,64]{3,1,2,0:T(8,128)(2,1)} %param.6) | copy-start | bytes 55300
  1.3 1.6 %copy-start.2 = (f32[9,1,64]{2,1,0:T(1,128)S(1)}, f32[9,1,64]{2,1,0:T(1,128)}, u32[]{:S(2)}) copy-start(f32[9,1,64]{2,1,0:T(1,128)} %weight_ref.1) | copy-start | bytes 6916
